TPU v7x, 256 devices: a whole 4x4x8 slice. The times are simulated.
256 devices in a mesh: grp: 2 (over x_hi), seq: 128 (over y, z, x_lo, core).
Axes of the slice: x: 4 (x_hi: 2, x_lo: 2; x = x_hi * 2 + x_lo), y: 4, z: 8, core: 2. Of those that a mesh axis runs over, the one named last changes fastest.
Arguments:
- teach_q: bfloat16 [2, 16384, 1536], P('grp', 'seq'), may hold values from -60 to 60
- teach_k: bfloat16 [2, 16384, 1536], P('grp', 'seq'), may hold values from -6 to 6
- teach_v: bfloat16 [2, 16384, 1536], P('grp', 'seq'), may hold values from -6 to 6
- teach_resid: bfloat16 [2, 16384, 1536], P('grp', 'seq'), may hold values from -1400 to 1400
- teach_out_w: bfloat16 [1536, 1536], P('grp'), may hold values from -0.15625 to 0.15625
- teach_head_w: bfloat16 [1536, 1024], P('grp'), may hold values from -0.4375 to 0.4375
- teach_head_bias: float32 [1024], replicated, may hold values from -6 to 6
- stud_q: bfloat16 [2, 16384, 1024], P('grp', 'seq'), may hold values from -60 to 60
- stud_k: bfloat16 [2, 16384, 1024], P('grp', 'seq'), may hold values from -6 to 6
- stud_v: bfloat16 [2, 16384, 1024], P('grp', 'seq'), may hold values from -6 to 6
- stud_resid: bfloat16 [2, 16384, 1024], P('grp', 'seq'), may hold values from -1400 to 1400
- stud_out_w: bfloat16 [1024, 1024], P('grp'), may hold values from -0.1875 to 0.1875
- stud_head_w: bfloat16 [1024, 1024], P('grp'), may hold values from -0.5 to 0.5
- stud_head_bias: float32 [1024], replicated, may hold values from -6 to 6
- lengths: int32 [2], replicated, may hold values from 8192 to 16384, as said below
- align: int32 [2, 16384], P('grp', 'seq'), may hold values from 0 to 16383, as said below
Outputs:
- grad_q: bfloat16 [2, 16384, 1024], P('grp', 'seq')
- grad_k: bfloat16 [2, 16384, 1024], P('grp', 'seq')
- grad_v: bfloat16 [2, 16384, 1024], P('grp', 'seq')
Inputs may be any that keep to these rules, and one draw needn't show every extreme that they name: `lengths`: one of the two utterances has all 16384 frames; the other is shorter. t - 16 <= align[g, t] <= t; in each row some frame has align[g, t] = t - 16.
All inputs are finite; a program needn't handle non-finite values.
Results may differ from a plain program's by a relative error of at most 0.023.
Values may be sent and summed in bfloat16 or wider, within the bound.
A program may use at most 128 MiB of HBM per device.

v0:
```python
import jax
import jax.numpy as jnp
from jax import lax
from jax.sharding import PartitionSpec as P

HD = 64
CTX = 512
MAXD = 16


score_scale = 0.125
grad_scale = 16.0
mask_fill = -1e30


def from_behind(x, axis, by):
    count = lax.axis_size(axis)
    pairs = [(i, i + by) for i in range(count) if 0 <= i + by < count]
    return lax.ppermute(x, axis, pairs)


def swapped_2(block, axis, apart):
    count = lax.axis_size(axis)
    route = []
    for low in range(count):
        high = low | 1 << apart
        if high != low and high < count:
            route += [(low, high), (high, low)]
    return lax.ppermute(block, axis, route)


def attend(query, keys, values, query_pos, key_pos, length):
    row_count = query.shape[0]
    key_count = keys.shape[0]
    head_count = query.shape[1] // HD
    query_heads = query.reshape(row_count, head_count, HD)
    key_heads = keys.reshape(key_count, head_count, HD)
    value_heads = values.reshape(key_count, head_count, HD)
    scores = (
        jnp.einsum("thd,shd->hts", query_heads, key_heads, preferred_element_type=jnp.float32)
        * score_scale
    )
    allowed = (key_pos[None, :] <= query_pos[:, None]) & (
        key_pos[None, :] >= query_pos[:, None] - CTX
    )
    allowed = allowed & (key_pos[None, :] >= 0) & (key_pos[None, :] < length)
    scores = jnp.where(allowed[None], scores, mask_fill)
    row_max = jnp.max(scores, axis=-1, keepdims=True)
    exp_scores = jnp.exp(scores - row_max)
    probs = exp_scores / jnp.sum(exp_scores, axis=-1, keepdims=True)
    rounded = probs.astype(jnp.bfloat16)
    context = jnp.einsum("hts,shd->thd", rounded, value_heads, preferred_element_type=jnp.float32)
    return (context.reshape(row_count, head_count * HD).astype(jnp.bfloat16), probs, rounded)


def on_device(
    teach_q,
    teach_k,
    teach_v,
    teach_resid,
    teach_out_w,
    teach_head_w,
    teach_head_bias,
    stud_q,
    stud_k,
    stud_v,
    stud_resid,
    stud_out_w,
    stud_head_w,
    stud_head_bias,
    lengths,
    align,
):
    teach_query = teach_q[0]
    teach_keys = teach_k[0]
    teach_values = teach_v[0]
    stud_query = stud_q[0]
    stud_keys = stud_k[0]
    stud_values = stud_v[0]
    frames_dev = teach_query.shape[0]
    reach = -(-CTX // frames_dev)
    group_index = lax.axis_index("grp")
    shard_index = lax.axis_index("seq")
    teach_len = jnp.take(lengths, group_index)
    stud_len = jnp.take(lengths, 1 - group_index)
    query_pos = shard_index * frames_dev + jnp.arange(frames_dev, dtype=jnp.int32)
    key_pos = (shard_index - reach) * frames_dev + jnp.arange(
        (reach + 1) * frames_dev, dtype=jnp.int32
    )
    earlier = []
    for distance in range(reach, 0, -1):
        earlier.append(
            from_behind((teach_keys, teach_values, stud_keys, stud_values), "seq", distance)
        )
    teach_key_all = jnp.concatenate([item[0] for item in earlier] + [teach_keys], axis=0)
    teach_value_all = jnp.concatenate([item[1] for item in earlier] + [teach_values], axis=0)
    stud_key_all = jnp.concatenate([item[2] for item in earlier] + [stud_keys], axis=0)
    stud_value_all = jnp.concatenate([item[3] for item in earlier] + [stud_values], axis=0)
    gathered = (
        lax.all_gather(teach_out_w, "grp", axis=0, tiled=True),
        lax.all_gather(teach_head_w, "grp", axis=0, tiled=True),
        lax.all_gather(stud_out_w, "grp", axis=0, tiled=True),
        lax.all_gather(stud_head_w, "grp", axis=0, tiled=True),
    )
    teach_out_full, teach_head_full, stud_out_full, stud_head_full = gathered
    teach_context, teach_probs, teach_rounded = attend(
        teach_query, teach_key_all, teach_value_all, query_pos, key_pos, teach_len
    )
    teach_hidden = (
        teach_resid[0].astype(jnp.float32)
        + jnp.dot(teach_context, teach_out_full, preferred_element_type=jnp.float32)
    ).astype(jnp.bfloat16)
    teach_logits = (
        jnp.dot(teach_hidden, teach_head_full, preferred_element_type=jnp.float32) + teach_head_bias
    )
    posterior = jax.nn.softmax(teach_logits, axis=-1).astype(jnp.bfloat16)
    swapped = swapped_2(posterior, "grp", 0)
    post_tail = from_behind(swapped[frames_dev - MAXD :], "seq", 1)
    extended = jnp.concatenate([post_tail, swapped], axis=0)
    local_rows = align[0] - (shard_index * frames_dev - MAXD)
    targets = jnp.take(extended, local_rows, axis=0).astype(jnp.float32)
    stud_context, stud_probs, stud_rounded = attend(
        stud_query, stud_key_all, stud_value_all, query_pos, key_pos, stud_len
    )
    stud_hidden = (
        stud_resid[0].astype(jnp.float32)
        + jnp.dot(stud_context, stud_out_full, preferred_element_type=jnp.float32)
    ).astype(jnp.bfloat16)
    stud_logits = (
        jnp.dot(stud_hidden, stud_head_full, preferred_element_type=jnp.float32) + stud_head_bias
    )
    predicted = jax.nn.softmax(stud_logits, axis=-1)
    valid_rows = (query_pos < stud_len).astype(jnp.float32)
    target_sum = jnp.sum(targets, axis=-1, keepdims=True)
    logit_grad = (grad_scale * valid_rows[:, None] * (target_sum * predicted - targets)).astype(
        jnp.bfloat16
    )
    hidden_grad = jnp.einsum(
        "tv,dv->td", logit_grad, stud_head_full, preferred_element_type=jnp.float32
    ).astype(jnp.bfloat16)
    mix_grad = jnp.einsum(
        "te,de->td", hidden_grad, stud_out_full, preferred_element_type=jnp.float32
    ).astype(jnp.bfloat16)
    head_count = stud_query.shape[1] // HD
    key_count = stud_key_all.shape[0]
    width = stud_query.shape[1]
    mix_heads = mix_grad.reshape(frames_dev, head_count, HD)
    value_heads = stud_value_all.reshape(key_count, head_count, HD)
    key_heads = stud_key_all.reshape(key_count, head_count, HD)
    query_heads = stud_query.reshape(frames_dev, head_count, HD)
    prob_grad = jnp.einsum(
        "thd,shd->hts", mix_heads, value_heads, preferred_element_type=jnp.float32
    )
    value_grad = jnp.einsum(
        "hts,thd->shd", stud_rounded, mix_heads, preferred_element_type=jnp.float32
    ).reshape(key_count, width)
    inner_sum = jnp.sum(stud_probs * prob_grad, axis=-1, keepdims=True)
    score_grad = (score_scale * stud_probs * (prob_grad - inner_sum)).astype(jnp.bfloat16)
    query_grad = jnp.einsum(
        "hts,shd->thd", score_grad, key_heads, preferred_element_type=jnp.float32
    )
    query_grad = query_grad.reshape(frames_dev, width).astype(jnp.bfloat16)
    key_grad = jnp.einsum(
        "hts,thd->shd", score_grad, query_heads, preferred_element_type=jnp.float32
    ).reshape(key_count, width)
    own_start = reach * frames_dev
    total_keys = key_grad[own_start:]
    total_values = value_grad[own_start:]
    for distance in range(1, reach + 1):
        row_start = (reach - distance) * frames_dev
        received = (
            from_behind(
                key_grad[row_start : row_start + frames_dev].astype(jnp.bfloat16), "seq", -distance
            ).astype(jnp.float32),
            from_behind(
                value_grad[row_start : row_start + frames_dev].astype(jnp.bfloat16),
                "seq",
                -distance,
            ).astype(jnp.float32),
        )
        total_keys = total_keys + received[0]
        total_values = total_values + received[1]
    return (
        query_grad[None],
        total_keys.astype(jnp.bfloat16)[None],
        total_values.astype(jnp.bfloat16)[None],
    )


def solution(mesh):
    return jax.shard_map(
        on_device,
        mesh=mesh,
        in_specs=(
            P("grp", "seq", None),
            P("grp", "seq", None),
            P("grp", "seq", None),
            P("grp", "seq", None),
            P("grp", None),
            P("grp", None),
            P(),
            P("grp", "seq", None),
            P("grp", "seq", None),
            P("grp", "seq", None),
            P("grp", "seq", None),
            P("grp", None),
            P("grp", None),
            P(),
            P(),
            P("grp", "seq"),
        ),
        out_specs=(P("grp", "seq", None), P("grp", "seq", None), P("grp", "seq", None)),
        check_vma=False,
    )
```

profile of v0, /device:TPU:24, one launch (start us, length us, event | category | flops | bytes accessed | tf_op | source)
XLA Modules:
  0.0 354.7 jit_solution(8499671837583138102)
XLA Ops:
  9.5 4.0 %collective-permute-start = (bf16[128,1024]{1,0:T(8,128)(2,1)}, bf16[128,1024]{1,0:T(8,128)(2,1)S(1)}, u32[]{:S(2)}, u32[]{:S(2)}) collective-permute-start(bf16[128,1024]{1,0:T(8,128)(2,1)} %bitcast), channel_id=1, source_target_pairs={{0,4},{1,5},{2,6},{3,7},{4,8},{5,9},{6,10},{7,11},{8,12},{9,13},{1... | collective-permute-start | bytes 786440 | tf_op jit(solution)/shard_map/ppermute | solution.py:19
  16.0 3.8 %collective-permute-start.2 = (bf16[128,1024]{1,0:T(8,128)(2,1)}, bf16[128,1024]{1,0:T(8,128)(2,1)}, u32[]{:S(2)}, u32[]{:S(2)}) collective-permute-start(bf16[128,1024]{1,0:T(8,128)(2,1)} %bitcast), channel_id=1, source_target_pairs={{0,2},{1,3},{2,4},{3,5},{4,6},{5,7},{6,8},{7,9},{8,10},{9,11},{10,... | collective-permute-start | bytes 786440 | tf_op jit(solution)/shard_map/ppermute | solution.py:19
  19.8 3.8 %collective-permute-start.8 = (bf16[128,1536]{1,0:T(8,128)(2,1)}, bf16[128,1536]{1,0:T(8,128)(2,1)}, u32[]{:S(2)}, u32[]{:S(2)}) collective-permute-start(bf16[128,1536]{1,0:T(8,128)(2,1)} %bitcast.20), channel_id=1, source_target_pairs={{0,4},{1,5},{2,6},{3,7},{4,8},{5,9},{6,10},{7,11},{8,12},{9,13},{1... | collective-permute-start | bytes 1179656 | tf_op jit(solution)/shard_map/ppermute | solution.py:19
  23.7 5.0 %collective-permute-start.14 = (bf16[128,1024]{1,0:T(8,128)(2,1)S(1)}, bf16[128,1024]{1,0:T(8,128)(2,1)}, u32[]{:S(2)}, u32[]{:S(2)}) collective-permute-start(bf16[128,1024]{1,0:T(8,128)(2,1)S(1)} %bitcast.172), channel_id=1, source_target_pairs={{0,4},{1,5},{2,6},{3,7},{4,8},{5,9},{6,10},{7,11},{8,12},{9,13},{1... | collective-permute-start | bytes 786440 | tf_op jit(solution)/shard_map/ppermute | solution.py:19
  38.8 10.9 %collective-permute-done.14 = bf16[128,1024]{1,0:T(8,128)(2,1)} collective-permute-done((bf16[128,1024]{1,0:T(8,128)(2,1)S(1)}, bf16[128,1024]{1,0:T(8,128)(2,1)}, u32[]{:S(2)}, u32[]{:S(2)}) %collective-permute-start.14) | collective-permute-done | bytes 262176 | tf_op jit(solution)/shard_map/ppermute | solution.py:19
  53.5 5.8 %collective-permute-start.15 = (bf16[128,1024]{1,0:T(8,128)(2,1)}, bf16[128,1024]{1,0:T(8,128)(2,1)}, u32[]{:S(2)}, u32[]{:S(2)}) collective-permute-start(bf16[128,1024]{1,0:T(8,128)(2,1)} %bitcast.169), channel_id=1, source_target_pairs={{0,3},{1,4},{2,5},{3,6},{4,7},{5,8},{6,9},{7,10},{8,11},{9,12},{10... | collective-permute-start | bytes 786440 | tf_op jit(solution)/shard_map/ppermute | solution.py:19
  60.5 3.9 %collective-permute-start.16 = (bf16[128,1024]{1,0:T(8,128)(2,1)}, bf16[128,1024]{1,0:T(8,128)(2,1)}, u32[]{:S(2)}, u32[]{:S(2)}) collective-permute-start(bf16[128,1024]{1,0:T(8,128)(2,1)} %bitcast.170), channel_id=1, source_target_pairs={{0,2},{1,3},{2,4},{3,5},{4,6},{5,7},{6,8},{7,9},{8,10},{9,11},{10,... | collective-permute-start | bytes 786440 | tf_op jit(solution)/shard_map/ppermute | solution.py:19
  72.0 4.3 %collective-permute-start.10 = (bf16[128,1536]{1,0:T(8,128)(2,1)}, bf16[128,1536]{1,0:T(8,128)(2,1)}, u32[]{:S(2)}, u32[]{:S(2)}) collective-permute-start(bf16[128,1536]{1,0:T(8,128)(2,1)} %bitcast.20), channel_id=1, source_target_pairs={{0,2},{1,3},{2,4},{3,5},{4,6},{5,7},{6,8},{7,9},{8,10},{9,11},{10,... | collective-permute-start | bytes 1179656 | tf_op jit(solution)/shard_map/ppermute | solution.py:19
  86.3 5.2 %fusion.59 = (f32[16,128]{1,0:T(8,128)S(1)}, f32[16,128,640]{1,2,0:T(8,128)}) fusion(pred[128,640]{0,1:T(8,128)(4,1)} %get-tuple-element.40, bf16[640,16,64]{0,2,1:T(8,128)(2,1)S(1)} %constant_dynamic-update-slice_fusion, bf16[128,16,64]{0,2,1:T(8,128)(2,1)S(1)} %bitcast.160), kind=kOutput, calls=%fused_computation.104 | convolution fusion | flops 173015680 | bytes 6905856 | tf_op jit(solution)/shard_map/sub | solution.py:49
  95.0 3.8 %collective-permute-start.5 = (bf16[128,1536]{1,0:T(8,128)(2,1)S(1)}, bf16[128,1536]{1,0:T(8,128)(2,1)S(1)}, u32[]{:S(2)}, u32[]{:S(2)}) collective-permute-start(bf16[128,1536]{1,0:T(8,128)(2,1)S(1)} %bitcast.164), channel_id=1, source_target_pairs={{0,3},{1,4},{2,5},{3,6},{4,7},{5,8},{6,9},{7,10},{8,11},{9,12},{10... | collective-permute-start | bytes 1179656 | tf_op jit(solution)/shard_map/ppermute | solution.py:19
  116.9 4.5 %collective-permute-done.6 = bf16[128,1536]{1,0:T(8,128)(2,1)} collective-permute-done((bf16[128,1536]{1,0:T(8,128)(2,1)S(1)}, bf16[128,1536]{1,0:T(8,128)(2,1)}, u32[]{:S(2)}, u32[]{:S(2)}) %collective-permute-start.6) | collective-permute-done | bytes 393248 | tf_op jit(solution)/shard_map/ppermute | solution.py:19
  127.5 7.5 %fusion.61 = (f32[24,128]{1,0:T(8,128)S(1)}, f32[24,128,640]{1,2,0:T(8,128)}) fusion(pred[128,640]{0,1:T(8,128)(4,1)S(1)} %get-tuple-element.39, bf16[640,24,64]{0,2,1:T(8,128)(2,1)} %constant_dynamic-update-slice_fusion.10, bf16[128,24,64]{0,2,1:T(8,128)(2,1)S(1)} %bitcast.167), kind=kOutput, calls=%fused_computation.106 | convolution fusion | flops 259523200 | bytes 10317824 | tf_op jit(solution)/shard_map/sub | solution.py:49
  135.8 4.6 %fusion.15 = bf16[24,64,128]{2,1,0:T(8,128)(2,1)S(1)} fusion(bf16[640,24,64]{0,2,1:T(8,128)(2,1)} %constant_dynamic-update-slice_fusion.5, f32[24,128,640]{1,2,0:T(8,128)} %get-tuple-element.48, f32[24,128]{1,0:T(8,128)S(1)} %get-tuple-element.47), kind=kOutput, calls=%fused_computation.27 | convolution fusion | flops 255787008 | bytes 10235904 | tf_op jit(solution)/shard_map/hts,shd->thd/dot_general | solution.py:52
  140.4 31.7 %all-gather.5.cloned.1.call-done = bf16[1536,1536]{1,0:T(8,128)(2,1)} async-done(((bf16[768,1536]{1,0:T(8,128)(2,1)}), bf16[1536,1536]{1,0:T(8,128)(2,1)}) %all-gather.5.cloned.1.call-update) | async-done | bytes 4718608 | tf_op jit(solution)/shard_map/all_gather | solution.py:100
  172.2 4.7 %fusion.62 = (f32[128]{0:T(128)S(1)}, f32[128,1024]{1,0:T(8,128)S(1)}) fusion(f32[1024]{0:T(1024)S(1)} %copy-done.11, bf16[1536,1024]{1,0:T(8,128)(2,1)} %all-gather.7.cloned.1.call-done, bf16[128,1536]{0,1:T(8,128)(2,1)S(1)} %bitcast.162, bf16[1536,1536]{1,0:T(8,128)(2,1)} %all-gather.5.cloned.1.call-done, bf16[1,128,1536]{2,1,0:T(8,128)(2,1)S(1)} %copy-done.2), kind=kOutput, calls=%fused_computation.107 | convolution fusion | flops 1007484800 | bytes 9179648 | tf_op jit(solution)/shard_map/dot_general | solution.py:114
  178.2 38.2 %all-gather.11.cloned.1.call-done = bf16[1024,1024]{1,0:T(8,128)(2,1)} async-done(((bf16[512,1024]{1,0:T(8,128)(2,1)}), bf16[1024,1024]{1,0:T(8,128)(2,1)}) %all-gather.11.cloned.1.call-update) | async-done | bytes 2097168 | tf_op jit(solution)/shard_map/all_gather | solution.py:103
  216.3 40.9 %all-gather.9.cloned.1.call-done = bf16[1024,1024]{1,0:T(8,128)(2,1)} async-done(((bf16[512,1024]{1,0:T(8,128)(2,1)}), bf16[1024,1024]{1,0:T(8,128)(2,1)}) %all-gather.9.cloned.1.call-update) | async-done | bytes 2097168 | tf_op jit(solution)/shard_map/all_gather | solution.py:102
  262.5 6.1 %collective-permute-done.13 = bf16[16,1024]{1,0:T(8,128)(2,1)S(1)} collective-permute-done((bf16[16,1024]{1,0:T(8,128)(2,1)S(1)}, bf16[16,1024]{1,0:T(8,128)(2,1)S(1)}, u32[]{:S(2)}, u32[]{:S(2)}) %collective-permute-start.13) | collective-permute-done | bytes 32800 | tf_op jit(solution)/shard_map/ppermute | solution.py:19
  269.7 3.8 %convolution_convert_fusion.1 = bf16[128,1024]{1,0:T(8,128)(2,1)S(1)} fusion(bf16[1024,1024]{1,0:T(8,128)(2,1)} %all-gather.9.cloned.1.call-done, bf16[1024,1024]{1,0:T(8,128)(2,1)} %all-gather.11.cloned.1.call-done, f32[128,1024]{1,0:T(8,128)S(1)} %get-tuple-element.46, f32[128]{0:T(128)S(1)} %fusion.27, f32[128]{0:T(128)S(1)} %get-tuple-element.45, ...), kind=kOutput, calls=%fused_computation.33 | convolution fusion | flops 538181632 | bytes 5245056 | tf_op jit(solution)/shard_map/te,de->td/dot_general | solution.py:141
  273.7 5.3 %fusion.64 = (bf16[640,16,64]{0,2,1:T(8,128)(2,1)S(1)}, f32[640,16,64]{0,2,1:T(8,128)}) fusion(bf16[128,16,64]{0,2,1:T(8,128)(2,1)S(1)} %bitcast.173, f32[16,128,640]{1,2,0:T(8,128)} %get-tuple-element.44, f32[16,128]{1,0:T(8,128)S(1)} %get-tuple-element.43), kind=kOutput, calls=%fused_computation.109 | convolution fusion | flops 171048960 | bytes 9445376 | tf_op jit(solution)/shard_map/hts,thd->shd/dot_general | solution.py:154
  298.5 5.1 %multiply_convert_fusion = bf16[16,128,640]{1,2,0:T(8,128)(2,1)S(1)} fusion(f32[16,128,640]{1,2,0:T(8,128)} %get-tuple-element.52, f32[16,128]{1,0:T(8,128)S(1)} %get-tuple-element.51, f32[16,128,640]{1,2,0:T(8,128)} %get-tuple-element.44, f32[16,128]{1,0:T(8,128)S(1)} %get-tuple-element.43), kind=kLoop, calls=%fused_computation.8 | loop fusion | flops 6553600 | bytes 13123584 | tf_op jit(solution)/shard_map/convert_element_type | solution.py:158
  323.3 4.3 %collective-permute-start.19 = (bf16[128,1024]{1,0:T(8,128)(2,1)}, bf16[128,1024]{1,0:T(8,128)(2,1)S(1)}, u32[]{:S(2)}, u32[]{:S(2)}) collective-permute-start(bf16[128,1024]{1,0:T(8,128)(2,1)} %copy.93), channel_id=1, source_target_pairs={{2,0},{3,1},{4,2},{5,3},{6,4},{7,5},{8,6},{9,7},{10,8},{11,9},{12,... | collective-permute-start | bytes 786440 | tf_op jit(solution)/shard_map/ppermute | solution.py:19
  336.7 5.6 %collective-permute-done.20 = bf16[128,1024]{1,0:T(8,128)(2,1)S(1)} collective-permute-done((bf16[128,1024]{1,0:T(8,128)(2,1)}, bf16[128,1024]{1,0:T(8,128)(2,1)S(1)}, u32[]{:S(2)}, u32[]{:S(2)}) %collective-permute-start.20) | collective-permute-done | bytes 262176 | tf_op jit(solution)/shard_map/ppermute | solution.py:19
  342.3 4.0 %collective-permute-done.21 = bf16[128,1024]{1,0:T(8,128)(2,1)S(1)} collective-permute-done((bf16[128,1024]{1,0:T(8,128)(2,1)}, bf16[128,1024]{1,0:T(8,128)(2,1)S(1)}, u32[]{:S(2)}, u32[]{:S(2)}) %collective-permute-start.21) | collective-permute-done | bytes 262176 | tf_op jit(solution)/shard_map/ppermute | solution.py:19
  (164 shorter events, 122.0 us)
Async XLA Ops:
  7.2 133.3 %all-gather.7.cloned.1.call-start = ((), (), s32[]{:S(2)}) async-start(), calls=%async_computation.1 | async-start | bytes 4718592 | tf_op jit(solution)/shard_map/all_gather | solution.py:101
  7.9 164.2 %all-gather.5.cloned.1.call-start = ((), (), s32[]{:S(2)}) async-start(), calls=%async_computation | async-start | bytes 7077888 | tf_op jit(solution)/shard_map/all_gather | solution.py:100
  8.7 207.6 %all-gather.11.cloned.1.call-start = ((), (), s32[]{:S(2)}) async-start(), calls=%async_computation.3 | async-start | bytes 3145728 | tf_op jit(solution)/shard_map/all_gather | solution.py:103
  9.4 247.8 %all-gather.9.cloned.1.call-start = ((), (), s32[]{:S(2)}) async-start(), calls=%async_computation.2 | async-start | bytes 3145728 | tf_op jit(solution)/shard_map/all_gather | solution.py:102
  9.5 26.5 %collective-permute-start = (bf16[128,1024]{1,0:T(8,128)(2,1)}, bf16[128,1024]{1,0:T(8,128)(2,1)S(1)}, u32[]{:S(2)}, u32[]{:S(2)}) collective-permute-start(bf16[128,1024]{1,0:T(8,128)(2,1)} %bitcast), channel_id=1, source_target_pairs={{0,4},{1,5},{2,6},{3,7},{4,8},{5,9},{6,10},{7,11},{8,12},{9,13},{1... | collective-permute-start | bytes 786440 | tf_op jit(solution)/shard_map/ppermute | solution.py:19
  13.5 40.1 %collective-permute-start.1 = (bf16[128,1024]{1,0:T(8,128)(2,1)}, bf16[128,1024]{1,0:T(8,128)(2,1)}, u32[]{:S(2)}, u32[]{:S(2)}) collective-permute-start(bf16[128,1024]{1,0:T(8,128)(2,1)} %bitcast), channel_id=1, source_target_pairs={{0,3},{1,4},{2,5},{3,6},{4,7},{5,8},{6,9},{7,10},{8,11},{9,12},{10... | collective-permute-start | bytes 786440 | tf_op jit(solution)/shard_map/ppermute | solution.py:19
  16.0 44.5 %collective-permute-start.2 = (bf16[128,1024]{1,0:T(8,128)(2,1)}, bf16[128,1024]{1,0:T(8,128)(2,1)}, u32[]{:S(2)}, u32[]{:S(2)}) collective-permute-start(bf16[128,1024]{1,0:T(8,128)(2,1)} %bitcast), channel_id=1, source_target_pairs={{0,2},{1,3},{2,4},{3,5},{4,6},{5,7},{6,8},{7,9},{8,10},{9,11},{10,... | collective-permute-start | bytes 786440 | tf_op jit(solution)/shard_map/ppermute | solution.py:19
  19.8 75.2 %collective-permute-start.8 = (bf16[128,1536]{1,0:T(8,128)(2,1)}, bf16[128,1536]{1,0:T(8,128)(2,1)}, u32[]{:S(2)}, u32[]{:S(2)}) collective-permute-start(bf16[128,1536]{1,0:T(8,128)(2,1)} %bitcast.20), channel_id=1, source_target_pairs={{0,4},{1,5},{2,6},{3,7},{4,8},{5,9},{6,10},{7,11},{8,12},{9,13},{1... | collective-permute-start | bytes 1179656 | tf_op jit(solution)/shard_map/ppermute | solution.py:19
  23.7 26.0 %collective-permute-start.14 = (bf16[128,1024]{1,0:T(8,128)(2,1)S(1)}, bf16[128,1024]{1,0:T(8,128)(2,1)}, u32[]{:S(2)}, u32[]{:S(2)}) collective-permute-start(bf16[128,1024]{1,0:T(8,128)(2,1)S(1)} %bitcast.172), channel_id=1, source_target_pairs={{0,4},{1,5},{2,6},{3,7},{4,8},{5,9},{6,10},{7,11},{8,12},{9,13},{1... | collective-permute-start | bytes 786440 | tf_op jit(solution)/shard_map/ppermute | solution.py:19
  36.0 71.4 %collective-permute-start.9 = (bf16[128,1536]{1,0:T(8,128)(2,1)}, bf16[128,1536]{1,0:T(8,128)(2,1)}, u32[]{:S(2)}, u32[]{:S(2)}) collective-permute-start(bf16[128,1536]{1,0:T(8,128)(2,1)} %bitcast.20), channel_id=1, source_target_pairs={{0,3},{1,4},{2,5},{3,6},{4,7},{5,8},{6,9},{7,10},{8,11},{9,12},{10... | collective-permute-start | bytes 1179656 | tf_op jit(solution)/shard_map/ppermute | solution.py:19
  49.7 18.6 %collective-permute-start.3 = (bf16[128,1024]{1,0:T(8,128)(2,1)}, bf16[128,1024]{1,0:T(8,128)(2,1)}, u32[]{:S(2)}, u32[]{:S(2)}) collective-permute-start(bf16[128,1024]{1,0:T(8,128)(2,1)} %bitcast), channel_id=1, source_target_pairs={{0,1},{1,2},{2,3},{3,4},{4,5},{5,6},{6,7},{7,8},{8,9},{9,10},{10,1... | collective-permute-start | bytes 786440 | tf_op jit(solution)/shard_map/ppermute | solution.py:19
  53.5 18.5 %collective-permute-start.15 = (bf16[128,1024]{1,0:T(8,128)(2,1)}, bf16[128,1024]{1,0:T(8,128)(2,1)}, u32[]{:S(2)}, u32[]{:S(2)}) collective-permute-start(bf16[128,1024]{1,0:T(8,128)(2,1)} %bitcast.169), channel_id=1, source_target_pairs={{0,3},{1,4},{2,5},{3,6},{4,7},{5,8},{6,9},{7,10},{8,11},{9,12},{10... | collective-permute-start | bytes 786440 | tf_op jit(solution)/shard_map/ppermute | solution.py:19
  72.0 39.6 %collective-permute-start.10 = (bf16[128,1536]{1,0:T(8,128)(2,1)}, bf16[128,1536]{1,0:T(8,128)(2,1)}, u32[]{:S(2)}, u32[]{:S(2)}) collective-permute-start(bf16[128,1536]{1,0:T(8,128)(2,1)} %bitcast.20), channel_id=1, source_target_pairs={{0,2},{1,3},{2,4},{3,5},{4,6},{5,7},{6,8},{7,9},{8,10},{9,11},{10,... | collective-permute-start | bytes 1179656 | tf_op jit(solution)/shard_map/ppermute | solution.py:19
  78.2 34.7 %collective-permute-start.11 = (bf16[128,1536]{1,0:T(8,128)(2,1)}, bf16[128,1536]{1,0:T(8,128)(2,1)}, u32[]{:S(2)}, u32[]{:S(2)}) collective-permute-start(bf16[128,1536]{1,0:T(8,128)(2,1)} %bitcast.20), channel_id=1, source_target_pairs={{0,1},{1,2},{2,3},{3,4},{4,5},{5,6},{6,7},{7,8},{8,9},{9,10},{10,1... | collective-permute-start | bytes 1179656 | tf_op jit(solution)/shard_map/ppermute | solution.py:19
  82.7 19.0 %collective-permute-start.4 = (bf16[128,1536]{1,0:T(8,128)(2,1)}, bf16[128,1536]{1,0:T(8,128)(2,1)}, u32[]{:S(2)}, u32[]{:S(2)}) collective-permute-start(bf16[128,1536]{1,0:T(8,128)(2,1)} %bitcast.163), channel_id=1, source_target_pairs={{0,4},{1,5},{2,6},{3,7},{4,8},{5,9},{6,10},{7,11},{8,12},{9,13},{1... | collective-permute-start | bytes 1179656 | tf_op jit(solution)/shard_map/ppermute | solution.py:19
  95.0 21.6 %collective-permute-start.5 = (bf16[128,1536]{1,0:T(8,128)(2,1)S(1)}, bf16[128,1536]{1,0:T(8,128)(2,1)S(1)}, u32[]{:S(2)}, u32[]{:S(2)}) collective-permute-start(bf16[128,1536]{1,0:T(8,128)(2,1)S(1)} %bitcast.164), channel_id=1, source_target_pairs={{0,3},{1,4},{2,5},{3,6},{4,7},{5,8},{6,9},{7,10},{8,11},{9,12},{10... | collective-permute-start | bytes 1179656 | tf_op jit(solution)/shard_map/ppermute | solution.py:19
  101.7 19.7 %collective-permute-start.6 = (bf16[128,1536]{1,0:T(8,128)(2,1)S(1)}, bf16[128,1536]{1,0:T(8,128)(2,1)}, u32[]{:S(2)}, u32[]{:S(2)}) collective-permute-start(bf16[128,1536]{1,0:T(8,128)(2,1)S(1)} %bitcast.165), channel_id=1, source_target_pairs={{0,2},{1,3},{2,4},{3,5},{4,6},{5,7},{6,8},{7,9},{8,10},{9,11},{10,... | collective-permute-start | bytes 1179656 | tf_op jit(solution)/shard_map/ppermute | solution.py:19
  107.3 18.1 %collective-permute-start.7 = (bf16[128,1536]{1,0:T(8,128)(2,1)S(1)}, bf16[128,1536]{1,0:T(8,128)(2,1)}, u32[]{:S(2)}, u32[]{:S(2)}) collective-permute-start(bf16[128,1536]{1,0:T(8,128)(2,1)S(1)} %bitcast.166), channel_id=1, source_target_pairs={{0,1},{1,2},{2,3},{3,4},{4,5},{5,6},{6,7},{7,8},{8,9},{9,10},{10,1... | collective-permute-start | bytes 1179656 | tf_op jit(solution)/shard_map/ppermute | solution.py:19
  177.3 83.0 %collective-permute-start.12 = (bf16[128,1024]{1,0:T(8,128)(2,1)S(1)}, bf16[128,1024]{1,0:T(8,128)(2,1)S(1)}, u32[]{:S(2)}, u32[]{:S(2)}) collective-permute-start(bf16[128,1024]{1,0:T(8,128)(2,1)S(1)} %divide_convert_fusion.4), channel_id=1, source_target_pairs={{0,128},{128,0},{1,129},{129,1},{2,130},{130,2},{3,131},{131,3},{4... | collective-permute-start | bytes 786440 | tf_op jit(solution)/shard_map/ppermute | solution.py:29
  283.7 39.6 %collective-permute-start.22 = (bf16[128,1024]{1,0:T(8,128)(2,1)}, bf16[128,1024]{1,0:T(8,128)(2,1)}, u32[]{:S(2)}, u32[]{:S(2)}) collective-permute-start(bf16[128,1024]{1,0:T(8,128)(2,1)} %copy.97), channel_id=1, source_target_pairs={{1,0},{2,1},{3,2},{4,3},{5,4},{6,5},{7,6},{8,7},{9,8},{10,9},{11,1... | collective-permute-start | bytes 786440 | tf_op jit(solution)/shard_map/ppermute | solution.py:19
  286.7 40.9 %collective-permute-start.23 = (bf16[128,1024]{1,0:T(8,128)(2,1)}, bf16[128,1024]{1,0:T(8,128)(2,1)}, u32[]{:S(2)}, u32[]{:S(2)}) collective-permute-start(bf16[128,1024]{1,0:T(8,128)(2,1)} %copy.99), channel_id=1, source_target_pairs={{2,0},{3,1},{4,2},{5,3},{6,4},{7,5},{8,6},{9,7},{10,8},{11,9},{12,... | collective-permute-start | bytes 786440 | tf_op jit(solution)/shard_map/ppermute | solution.py:19
  290.0 40.8 %collective-permute-start.24 = (bf16[128,1024]{1,0:T(8,128)(2,1)}, bf16[128,1024]{1,0:T(8,128)(2,1)}, u32[]{:S(2)}, u32[]{:S(2)}) collective-permute-start(bf16[128,1024]{1,0:T(8,128)(2,1)} %copy.100), channel_id=1, source_target_pairs={{3,0},{4,1},{5,2},{6,3},{7,4},{8,5},{9,6},{10,7},{11,8},{12,9},{13... | collective-permute-start | bytes 786440 | tf_op jit(solution)/shard_map/ppermute | solution.py:19
  294.0 40.0 %collective-permute-start.25 = (bf16[128,1024]{1,0:T(8,128)(2,1)}, bf16[128,1024]{1,0:T(8,128)(2,1)}, u32[]{:S(2)}, u32[]{:S(2)}) collective-permute-start(bf16[128,1024]{1,0:T(8,128)(2,1)} %copy.101), channel_id=1, source_target_pairs={{4,0},{5,1},{6,2},{7,3},{8,4},{9,5},{10,6},{11,7},{12,8},{13,9},{1... | collective-permute-start | bytes 786440 | tf_op jit(solution)/shard_map/ppermute | solution.py:19
  309.1 27.0 %collective-permute-start.18 = (bf16[128,1024]{1,0:T(8,128)(2,1)}, bf16[128,1024]{1,0:T(8,128)(2,1)}, u32[]{:S(2)}, u32[]{:S(2)}) collective-permute-start(bf16[128,1024]{1,0:T(8,128)(2,1)} %copy.91), channel_id=1, source_target_pairs={{1,0},{2,1},{3,2},{4,3},{5,4},{6,5},{7,6},{8,7},{9,8},{10,9},{11,1... | collective-permute-start | bytes 786440 | tf_op jit(solution)/shard_map/ppermute | solution.py:19
  (23 other events, 517.1 us)
Sparse Core Ops, SparseCore 0:
  9.8 64.3 all-gather.6
  76.0 96.0 all-gather.4
  174.0 42.3 all-gather.10
  218.0 39.1 all-gather.8
where the time goes:
time: 356 us; the launch traced here: 355 us
  waiting for transfers between devices  150 us (42%)
  starting transfers between devices  81.2 us (23%)
  local copies, waits for them, and re-layouts  50.6 us (14%)
  matrix products  45.8 us (13%)
  between operations  15.9 us (4%)
  other arithmetic  11.3 us (3%)
    ppermute x25, starting transfers between devices, from_behind(): return lax.ppermute(x, axis, pairs)  80.1 us
    all_gather x1, waiting for transfers between devices, on_device(): lax.all_gather(stud_out_w, 'grp', axis=0, tiled=True)  40.9 us
    all_gather x1, waiting for transfers between devices, on_device(): lax.all_gather(stud_head_w, 'grp', axis=0, tiled=True)  38.2 us
    ppermute x25, waiting for transfers between devices, from_behind(): return lax.ppermute(x, axis, pairs)  37.2 us
    all_gather x1, waiting for transfers between devices, on_device(): lax.all_gather(teach_out_w, 'grp', axis=0, tiled=True)  31.7 us
    ppermute x16, local copies, waits for them, and re-layouts, from_behind(): return lax.ppermute(x, axis, pairs)  15.8 us
    unnamed x57, local copies, waits for them, and re-layouts  14.5 us
    sub x2, matrix products, attend(): exp_scores = jnp.exp(scores - row_max)  12.7 us
  transfers between devices with their start and end apart: 30, of which 13 were waited for; matrix products, arithmetic and copies ran while one was open for 26% of the time, Pallas kernels for 0%

commit v1 on v0

v1 whole, which is shorter than its diff:
```python
import functools

import jax
import jax.numpy as jnp
from jax import lax
from jax.experimental import pallas as pl
from jax.experimental.pallas import tpu as pltpu
from jax.sharding import PartitionSpec as P

CTX = 512
MAXD = 16
R = 128
WIN = CTX + R
DT = 1536
DS = 1024
VOCAB = 1024
TP = DT // 128
SP = DS // 128
CW = 256
PPC = CW // 128
TCH = DT // CW
SCH = DS // CW
NCH = TCH + SCH
NY = 4

FILL = -1e30
F32 = jnp.float32
BF16 = jnp.bfloat16
MESH = pl.DeviceIdType.MESH
NT = (((1,), (1,)), ((), ()))
NN = (((1,), (0,)), ((), ()))


def mm(a, b, dims=NN):
    return lax.dot_general(a, b, dims, preferred_element_type=F32)


def cols(i, width):
    return pl.ds(pl.multiple_of(i * width, width), width)


class Cast:
    def __init__(self, place, send, recv, group, seq, zdev, xdev, cdev, xl, core):
        self.place, self.send, self.recv = place, send, recv
        self.g, self.zdev, self.xdev, self.cdev = group, zdev, xdev, cdev
        self.xl, self.core = xl, core

    def copy(self, kind, chunk):
        if kind == 0:
            src, dst, dev = 0, 4, self.zdev
        elif kind == 1:
            src, dst, dev = 4 * self.xl, 2, self.xdev
        elif kind == 2:
            src, dst, dev = 4 * self.core, 1 + 2 * self.core, self.cdev
        else:
            src, dst, dev = 2, 3 - 2 * self.core, self.cdev
        return pltpu.make_async_remote_copy(
            src_ref=self.place(src, chunk),
            dst_ref=self.place(dst, chunk),
            send_sem=self.send.at[kind, chunk],
            recv_sem=self.recv.at[kind, chunk],
            device_id=(self.g, dev),
            device_id_type=MESH,
        )

    def start(self, chunk):
        self.copy(0, chunk).start()

    def landed(self, kind, chunk):
        dist = (4, 2, 3 - 2 * self.core, 1 + 2 * self.core)[kind]
        ref = self.place(dist, chunk)
        pltpu.make_async_remote_copy(
            src_ref=ref,
            dst_ref=ref,
            send_sem=self.send.at[kind, chunk],
            recv_sem=self.recv.at[kind, chunk],
            device_id=(self.g, self.cdev),
            device_id_type=MESH,
        ).wait_recv()

    def a(self, chunk):
        self.landed(0, chunk)
        self.copy(1, chunk).start()
        self.copy(2, chunk).start()

    def b(self, chunk):
        self.landed(1, chunk)
        self.copy(3, chunk).start()

    def c(self, chunk):
        self.landed(2, chunk)
        self.landed(3, chunk)

    def sent(self, chunk):
        for kind in range(4):
            self.copy(kind, chunk).wait_send()


def kernel(
    ns,
    tq,
    tk,
    tv,
    tr,
    tow,
    thw,
    thb,
    sq,
    sk,
    sv,
    sr,
    sow,
    shw,
    shb,
    lens,
    align,
    gq,
    gk,
    gv,
    kv,
    qt,
    rt,
    rs,
    wt,
    ws,
    qm,
    probs,
    ctx_t,
    ctx_s,
    mix_s,
    hid,
    logits,
    post,
    ext,
    tail,
    lgrad,
    bias_t,
    bias_s,
    bias_k,
    stat_c,
    stat,
    lsem,
    kv_send,
    kv_recv,
    q_send,
    q_recv,
    m_send,
    m_recv,
    s_send,
    s_recv,
    wx_send,
    wx_recv,
    wy_send,
    wy_recv,
    wc_send,
    wc_recv,
    p_send,
    p_recv,
):
    g = lax.axis_index("grp")
    s = lax.axis_index("seq")
    og = 1 - g
    core = lax.rem(s, 2)
    xl = lax.rem(s // 2, 2)
    ystep = ns // NY
    y = s // ystep
    xdev = s + 2 - 4 * xl
    cdev = s + 1 - 2 * core
    ahead = lax.rem(s + 4, ns)
    behind = lax.rem(s + ns - 4, ns)
    ynext = lax.rem(s + ystep, ns)
    yprev = lax.rem(s + ns - ystep, ns)
    s_next = lax.rem(s + 1, ns)
    s_prev = lax.rem(s + ns - 1, ns)

    own = [
        (tk.at[0], kv.at[0, pl.ds(CTX, R), pl.ds(0, DT)]),
        (tv.at[0], kv.at[1, pl.ds(CTX, R), pl.ds(0, DT)]),
        (sk.at[0], kv.at[0, pl.ds(CTX, R), pl.ds(DT, DS)]),
        (sv.at[0], kv.at[1, pl.ds(CTX, R), pl.ds(DT, DS)]),
        (sq.at[0], qm.at[0, pl.ds(0, R), :]),
        (tq.at[0], qt),
        (tr.at[0], rt),
        (sr.at[0], rs),
        (tow, wt.at[pl.ds(pl.multiple_of(g * (DT // 2), DT // 2), DT // 2), pl.ds(0, DT)]),
        (thw, wt.at[pl.ds(pl.multiple_of(g * (DT // 2), DT // 2), DT // 2), pl.ds(DT, VOCAB)]),
        (sow, ws.at[pl.ds(pl.multiple_of(g * (DS // 2), DS // 2), DS // 2), pl.ds(0, DS)]),
        (shw, ws.at[pl.ds(pl.multiple_of(g * (DS // 2), DS // 2), DS // 2), pl.ds(DS, VOCAB)]),
    ]
    local = [pltpu.make_async_copy(a, b, lsem.at[i]) for i, (a, b) in enumerate(own)]
    for item in local:
        item.start()
    tail[pl.ds(MAXD, R - MAXD), :] = jnp.zeros((R - MAXD, VOCAB), BF16)

    barrier = pltpu.get_barrier_semaphore()
    peers = [
        (g, xdev),
        (g, cdev),
        (g, ahead),
        (g, behind),
        (g, ynext),
        (g, yprev),
        (og, xdev),
        (og, s),
        (og, s_next),
        (og, s_prev),
    ]
    for peer in peers:
        pl.semaphore_signal(barrier, inc=1, device_id=peer, device_id_type=MESH)
    pl.semaphore_wait(barrier, len(peers))

    def kv_place(dist, chunk):
        return kv.at[:, cols(4 - dist, R), cols(chunk, CW)]

    def q_place(dist, chunk):
        return qm.at[0, cols(dist, R), :]

    def m_place(dist, chunk):
        return qm.at[1, cols(dist, R), cols(chunk, CW)]

    def s_place(dist, chunk):
        return stat.at[:, cols(dist, R)]

    kvc = Cast(kv_place, kv_send, kv_recv, g, s, ahead, xdev, cdev, xl, core)
    back = (g, s, behind, xdev, cdev, 1 - xl, 1 - core)
    qc = Cast(q_place, q_send, q_recv, *back)
    mc = Cast(m_place, m_send, m_recv, *back)
    sc = Cast(s_place, s_send, s_recv, *back)

    def piece(group, owner_y, of, lo=0, n=None):
        depth = (DT if of < 2 else DS) // 16
        half = (DT if of < 2 else DS) // 2
        n = depth if n is None else n
        first = group * half + (owner_y * 2 + core) * depth + lo
        rows = pl.ds(pl.multiple_of(first, 16), n)
        if of == 0:
            return wt.at[rows, pl.ds(0, DT)]
        if of == 1:
            return wt.at[rows, pl.ds(DT, VOCAB)]
        return ws.at[rows, :]

    def across(i):
        source = (tow, thw, sow, shw)[i]
        depth = (DT if i < 2 else DS) // 16
        half = (DT if i < 2 else DS) // 2
        rows = pl.ds(pl.multiple_of((y * 2 + core) * depth, 16), depth)
        there = pl.ds(pl.multiple_of(g * half + (y * 2 + core) * depth, 16), depth)
        dest = (
            wt.at[there, pl.ds(0, DT)],
            wt.at[there, pl.ds(DT, VOCAB)],
            ws.at[there, pl.ds(0, DS)],
            ws.at[there, pl.ds(DS, VOCAB)],
        )[i]
        return pltpu.make_async_remote_copy(
            src_ref=source.at[rows, :],
            dst_ref=dest,
            send_sem=wx_send.at[i],
            recv_sem=wx_recv.at[i],
            device_id=(og, xdev),
            device_id_type=MESH,
        )

    def along(kind, of):
        depth = (DT if of < 2 else DS) // 16
        if kind < 2:
            ref = piece(og, y, of)
        elif kind == 2:
            ref = piece(og, lax.rem(y + NY - 1, NY), of, 0, depth // 2)
        else:
            ref = piece(og, lax.rem(y + 1, NY), of, depth // 2, depth // 2)
        return pltpu.make_async_remote_copy(
            src_ref=ref,
            dst_ref=ref,
            send_sem=wy_send.at[kind, of],
            recv_sem=wy_recv.at[kind, of],
            device_id=(g, (ynext, yprev)[kind % 2]),
            device_id_type=MESH,
        )

    def other_core(step, of):
        ref = piece(og, lax.rem(y + step, NY), of)
        return pltpu.make_async_remote_copy(
            src_ref=ref,
            dst_ref=ref,
            send_sem=wc_send.at[step, of],
            recv_sem=wc_recv.at[step, of],
            device_id=(g, cdev),
            device_id_type=MESH,
        )

    def w_first(of):
        if of < 2:
            across(of).wait_recv()
        else:
            across(2).wait_recv()
            across(3).wait_recv()
        along(0, of).start()
        along(1, of).start()
        other_core(0, of).start()

    def w_second(of):
        along(0, of).wait_recv()
        along(1, of).wait_recv()
        along(2, of).start()
        along(3, of).start()
        other_core(1, of).start()
        other_core(3, of).start()

    def w_third(of):
        along(2, of).wait_recv()
        along(3, of).wait_recv()
        other_core(2, of).start()

    def w_ready(of):
        for step in range(NY):
            other_core(step, of).wait_recv()

    for i in range(4):
        across(i).start()
    local[0].wait()
    local[1].wait()
    for c in range(TCH):
        kvc.start(c)
    local[2].wait()
    local[3].wait()
    for c in range(TCH, NCH):
        kvc.start(c)
    local[4].wait()
    qc.start(0)
    for item in local[5:]:
        item.wait()

    row = lax.broadcasted_iota(jnp.int32, (R, WIN), 0)
    col = lax.broadcasted_iota(jnp.int32, (R, WIN), 1)
    band = (col >= row) & (col <= row + CTX)
    first = s * R
    t_len = lens[g]
    s_len = lens[og]
    key_pos = first - CTX + col
    seen = band & (key_pos >= 0)
    bias_t[...] = jnp.where(seen & (key_pos < t_len), 0.0, FILL)
    bias_s[...] = jnp.where(seen & (key_pos < s_len), 0.0, FILL)
    bias_k[...] = jnp.where(band & (first + col < ns * R) & (first + row < s_len), 0.0, FILL)
    stat_c[...] = jnp.zeros_like(stat_c)

    lane = lax.broadcasted_iota(jnp.int32, (R, 128), 1)
    low = lane < 64

    def stacked(x):
        zero = jnp.zeros_like(x)
        return jnp.concatenate([jnp.where(low, x, zero), jnp.where(low, zero, x)], axis=0)

    def merged(x):
        return jnp.where(low, x[:R], x[R:])

    def scores(q, k, bias):
        sc2 = mm(stacked(q * 0.125), k, NT)
        return sc2.reshape(2, R, WIN) + bias[None]

    def teacher_pair(p):
        at = cols(p, 128)
        x = scores(qt[:, at], kv[0, :, at], bias_t[...])
        top = jnp.max(x, axis=-1, keepdims=True)
        e = jnp.exp(x - top)
        inv = 1.0 / jnp.sum(e, axis=-1, keepdims=True)
        o = mm(e.astype(BF16).reshape(2 * R, WIN), kv[1, :, at])
        o = o * inv.reshape(2 * R, 1)
        ctx_t[:, at] = merged(o).astype(BF16)

    kvc.a(0)

    def teacher_chunk(c, carry):
        kvc.a(c + 1)
        kvc.b(c)

        @pl.when(c == 1)
        def _():
            w_first(0)

        @pl.when(c == 2)
        def _():
            w_first(1)

        @pl.when(c == 3)
        def _():
            w_second(0)

        @pl.when(c == 4)
        def _():
            w_first(2)
            w_third(0)

        @pl.when(c == 5)
        def _():
            w_second(1)

        kvc.c(c)
        for i in range(PPC):
            teacher_pair(c * PPC + i)
        return carry

    lax.fori_loop(0, TCH, teacher_chunk, 0)

    def project(n, tiles, fn):
        def body(i, carry):
            fn(i)
            return carry

        lax.fori_loop(0, tiles, body, 0)

    w_ready(0)

    def t_hidden(i):
        at = cols(i, 256)
        hid[:, at] = (rt[:, at].astype(F32) + mm(ctx_t[...], wt[:, at])).astype(BF16)

    project(0, DT // 256, t_hidden)
    kvc.a(TCH + 1)
    kvc.b(TCH)
    w_third(1)
    w_ready(1)

    def t_logits(i):
        at = cols(i, 256)
        logits[:, at] = mm(hid[...], wt[:, pl.ds(pl.multiple_of(DT + i * 256, 256), 256)]) + thb[:, at]

    project(0, VOCAB // 256, t_logits)
    x = logits[...]
    e = jnp.exp(x - jnp.max(x, axis=-1, keepdims=True))
    post[...] = (e * (1.0 / jnp.sum(e, axis=-1, keepdims=True))).astype(BF16)
    to_body = pltpu.make_async_remote_copy(
        src_ref=post,
        dst_ref=ext,
        send_sem=p_send.at[0],
        recv_sem=p_recv.at[0],
        device_id=(og, s),
        device_id_type=MESH,
    )
    to_tail = pltpu.make_async_remote_copy(
        src_ref=post.at[pl.ds(R - MAXD, MAXD), :],
        dst_ref=tail.at[pl.ds(0, MAXD), :],
        send_sem=p_send.at[1],
        recv_sem=p_recv.at[1],
        device_id=(og, s_next),
        device_id_type=MESH,
    )
    to_body.start()
    to_tail.start()

    def student_pair(j):
        at = cols(TP + j, 128)
        x = scores(qm[0, pl.ds(0, R), cols(j, 128)], kv[0, :, at], bias_s[...])
        top = jnp.max(x, axis=-1, keepdims=True)
        e = jnp.exp(x - top)
        total = jnp.sum(e, axis=-1, keepdims=True)
        pr = e * (1.0 / total)
        probs[j] = pr
        o = mm(pr.astype(BF16).reshape(2 * R, WIN), kv[1, :, at])
        o = merged(o)
        mix_s[:, cols(j, 128)] = o
        ctx_s[:, cols(j, 128)] = o.astype(BF16)
        lse = top + jnp.log(total)
        st = stat_c[...]
        st = jnp.where(lane == 2 * j, lse[0], st)
        stat_c[...] = jnp.where(lane == 2 * j + 1, lse[1], st)

    def student_chunk(c, carry):
        @pl.when(c < NCH - 1)
        def _():
            kvc.a(c + 1)

        kvc.b(c)

        @pl.when(c == TCH + 1)
        def _():
            w_second(2)
            qc.a(0)

        @pl.when(c == TCH + 2)
        def _():
            qc.b(0)

        @pl.when(c == TCH + 3)
        def _():
            w_third(2)

        kvc.c(c)
        for i in range(PPC):
            student_pair((c - TCH) * PPC + i)
        return carry

    kvc.c(TCH)
    for i in range(PPC):
        student_pair(i)
    lax.fori_loop(TCH + 1, NCH, student_chunk, 0)

    w_ready(2)

    def s_hidden(i):
        at = cols(i, 256)
        hid[:, at] = (rs[:, at].astype(F32) + mm(ctx_s[...], ws[:, at])).astype(BF16)

    project(0, DS // 256, s_hidden)

    def s_logits(i):
        at = cols(i, 256)
        w = ws[:, pl.ds(pl.multiple_of(DS + i * 256, 256), 256)]
        logits[:, at] = mm(hid[:, pl.ds(0, DS)], w) + shb[:, at]

    project(0, VOCAB // 256, s_logits)

    rows = jnp.broadcast_to(align[...], (R, R)).T - first
    pick_body = jnp.where(rows == lane, 1.0, 0.0).astype(BF16)
    pick_tail = jnp.where(rows + MAXD == lane, 1.0, 0.0)
    pick_tail = jnp.where(lane < MAXD, pick_tail, 0.0).astype(BF16)
    to_body.wait_recv()
    to_tail.wait_recv()
    targets = mm(pick_body, ext[...]) + mm(pick_tail, tail[...])
    x = logits[...]
    e = jnp.exp(x - jnp.max(x, axis=-1, keepdims=True))
    predicted = e * (1.0 / jnp.sum(e, axis=-1, keepdims=True))
    frame = first + lax.broadcasted_iota(jnp.int32, (R, 1), 0)
    valid = jnp.where(frame < s_len, 16.0, 0.0)
    total = jnp.sum(targets, axis=-1, keepdims=True)
    lgrad[...] = (valid * (total * predicted - targets)).astype(BF16)

    def s_hidden_grad(i):
        at = cols(i, 256)
        hid[:, at] = mm(lgrad[...], ws[at, pl.ds(DS, VOCAB)], NT).astype(BF16)

    project(0, DS // 256, s_hidden_grad)

    def s_mix_grad(i):
        at = cols(i, CW)
        qm[1, pl.ds(0, R), at] = mm(hid[:, pl.ds(0, DS)], ws[at, pl.ds(0, DS)], NT).astype(BF16)
        mc.start(i)

    project(0, DS // CW, s_mix_grad)

    def inner_pair(j, carry):
        at = cols(j, 128)
        prod = qm[1, pl.ds(0, R), at].astype(F32) * mix_s[:, at]
        zero = jnp.zeros_like(prod)
        in0 = jnp.sum(jnp.where(low, prod, zero), axis=-1, keepdims=True)
        in1 = jnp.sum(jnp.where(low, zero, prod), axis=-1, keepdims=True)
        st = stat_c[...]
        st = jnp.where(lane == 16 + 2 * j, in0, st)
        stat_c[...] = jnp.where(lane == 17 + 2 * j, in1, st)
        return carry

    lax.fori_loop(0, SP, inner_pair, 0)
    stat[:, pl.ds(0, R)] = stat_c[...].T[:32]
    sc.start(0)

    def query_pair(j):
        at = cols(j, 128)
        kat = cols(TP + j, 128)
        m = qm[1, pl.ds(0, R), at]
        dp = mm(stacked(m), kv[1, :, kat], NT).reshape(2, R, WIN)
        st = stat_c[...]
        zero = jnp.zeros_like(st)
        in0 = jnp.sum(jnp.where(lane == 16 + 2 * j, st, zero), axis=-1, keepdims=True)
        in1 = jnp.sum(jnp.where(lane == 17 + 2 * j, st, zero), axis=-1, keepdims=True)
        inner = jnp.concatenate([in0[None], in1[None]], axis=0)
        ds = (probs[j] * (dp - inner)).astype(BF16).reshape(2 * R, WIN)
        gq[0, :, at] = (merged(mm(ds, kv[0, :, kat])) * 0.125).astype(BF16)

    def query_chunk(c, carry):
        for i in range(PPC):
            query_pair(c * PPC + i)
        mc.a(c)

        @pl.when(c == 0)
        def _():
            sc.a(0)

        @pl.when(c == 1)
        def _():
            sc.b(0)

        @pl.when(c > 0)
        def _():
            mc.b(c - 1)

        return carry

    lax.fori_loop(0, SCH, query_chunk, 0)
    mc.b(SCH - 1)
    qc.c(0)
    sc.c(0)

    def key_pair(j):
        at = cols(j, 128)
        kat = cols(TP + j, 128)
        q = qm[0, :, at]
        m = qm[1, :, at]
        x = scores(kv[0, pl.ds(CTX, R), kat], q, bias_k[...])
        lse = jnp.concatenate([stat[pl.ds(2 * j, 1), :][None], stat[pl.ds(2 * j + 1, 1), :][None]], 0)
        inner = jnp.concatenate(
            [stat[pl.ds(16 + 2 * j, 1), :][None], stat[pl.ds(17 + 2 * j, 1), :][None]], 0
        )
        pr = jnp.exp(x - lse)
        gv[0, :, at] = merged(mm(pr.astype(BF16).reshape(2 * R, WIN), m)).astype(BF16)
        dp = mm(stacked(kv[1, pl.ds(CTX, R), kat]), m, NT).reshape(2, R, WIN)
        ds = (pr * (dp - inner)).astype(BF16).reshape(2 * R, WIN)
        gk[0, :, at] = (merged(mm(ds, q)) * 0.125).astype(BF16)

    def key_chunk(c, carry):
        mc.c(c)
        for i in range(PPC):
            key_pair(c * PPC + i)
        return carry

    lax.fori_loop(0, SCH, key_chunk, 0)

    def kv_sent(c, carry):
        kvc.sent(c)
        return carry

    lax.fori_loop(0, NCH, kv_sent, 0)

    def m_sent(c, carry):
        mc.sent(c)
        return carry

    lax.fori_loop(0, SCH, m_sent, 0)
    qc.sent(0)
    sc.sent(0)
    to_body.wait_send()
    to_tail.wait_send()
    for i in range(4):
        across(i).wait_send()
    for of in range(3):
        for kind in range(4):
            along(kind, of).wait_send()
        for step in range(NY):
            other_core(step, of).wait_send()


def on_device(*args):
    ns = lax.axis_size("seq")
    args = list(args)
    args[6] = args[6].reshape(1, VOCAB)
    args[13] = args[13].reshape(1, VOCAB)
    hbm = pl.BlockSpec(memory_space=pl.ANY)
    vmem = pl.BlockSpec(memory_space=pltpu.VMEM)
    smem = pl.BlockSpec(memory_space=pltpu.SMEM)
    in_specs = [hbm] * 16
    in_specs[6] = vmem
    in_specs[13] = vmem
    in_specs[14] = smem
    in_specs[15] = vmem
    out = jax.ShapeDtypeStruct((1, R, DS), BF16)
    dma = pltpu.SemaphoreType.DMA
    return pl.pallas_call(
        functools.partial(kernel, ns),
        out_shape=(out, out, out),
        in_specs=in_specs,
        out_specs=(vmem, vmem, vmem),
        scratch_shapes=[
            pltpu.VMEM((2, WIN, DT + DS), BF16),
            pltpu.VMEM((R, DT), BF16),
            pltpu.VMEM((R, DT), BF16),
            pltpu.VMEM((R, DS), BF16),
            pltpu.VMEM((DT, DT + VOCAB), BF16),
            pltpu.VMEM((DS, DS + VOCAB), BF16),
            pltpu.VMEM((2, WIN, DS), BF16),
            pltpu.VMEM((SP, 2, R, WIN), F32),
            pltpu.VMEM((R, DT), BF16),
            pltpu.VMEM((R, DS), BF16),
            pltpu.VMEM((R, DS), F32),
            pltpu.VMEM((R, DT), BF16),
            pltpu.VMEM((R, VOCAB), F32),
            pltpu.VMEM((R, VOCAB), BF16),
            pltpu.VMEM((R, VOCAB), BF16),
            pltpu.VMEM((R, VOCAB), BF16),
            pltpu.VMEM((R, VOCAB), BF16),
            pltpu.VMEM((R, WIN), F32),
            pltpu.VMEM((R, WIN), F32),
            pltpu.VMEM((R, WIN), F32),
            pltpu.VMEM((R, 128), F32),
            pltpu.VMEM((32, WIN), F32),
            dma((12,)),
            dma((4, NCH)),
            dma((4, NCH)),
            dma((4, 1)),
            dma((4, 1)),
            dma((4, SCH)),
            dma((4, SCH)),
            dma((4, 1)),
            dma((4, 1)),
            dma((4,)),
            dma((4,)),
            dma((4, 3)),
            dma((4, 3)),
            dma((4, 3)),
            dma((4, 3)),
            dma((2,)),
            dma((2,)),
        ],
        compiler_params=pltpu.CompilerParams(
            collective_id=0, has_side_effects=True, vmem_limit_bytes=56 * 1024 * 1024
        ),
    )(*args)


def solution(mesh):
    return jax.shard_map(
        on_device,
        mesh=mesh,
        in_specs=(
            P("grp", "seq", None),
            P("grp", "seq", None),
            P("grp", "seq", None),
            P("grp", "seq", None),
            P("grp", None),
            P("grp", None),
            P(),
            P("grp", "seq", None),
            P("grp", "seq", None),
            P("grp", "seq", None),
            P("grp", "seq", None),
            P("grp", None),
            P("grp", None),
            P(),
            P(),
            P("grp", "seq"),
        ),
        out_specs=(P("grp", "seq", None), P("grp", "seq", None), P("grp", "seq", None)),
        check_vma=False,
    )
```

time: 356 us -> 117 us (0.33)
  the two profiles are of different devices: /device:TPU:24 before, /device:TPU:1 now
where the time goes in v1:
time: 117 us
  Pallas kernels  111 us (95%)
  local copies, waits for them, and re-layouts  5.01 us (4%)
    pallas_call x1, Pallas kernels, on_device(): pl.pallas_call(functools.partial(kernel, ns), out_shape=(out, out, out),...  111 us
    unnamed x3, local copies, waits for them, and re-layouts  5.01 us

profile of v1, /device:TPU:1, one launch (start us, length us, event | category | flops | bytes accessed | tf_op | source)
XLA Modules:
  0.0 116.8 jit_solution(13989302736270515523)
XLA Ops:
  0.6 111.1 %shard_map.175 = (bf16[1,128,1024]{2,1,0:T(8,128)(2,1)}, bf16[1,128,1024]{2,1,0:T(8,128)(2,1)}, bf16[1,128,1024]{2,1,0:T(8,128)(2,1)}) custom-call(bf16[1,128,1536]{2,1,0:T(8,128)(2,1)} %tq.1, bf16[1,128,1536]{2,1,0:T(8,128)(2,1)} %tk.1, bf16[1,128,1536]{2,1,0:T(8,128)(2,1)} %tv.1, bf16[1,128,1536]{2,1,0:T(8,128)(2,1)} %tr.1, bf16[768,1536]{1,0:T(8,128)(2,1)} %tow.1, ...), custom_call_target="tpu_custom_call" | custom-call | tf_op jit(solution)/shard_map/pallas_call | solution.py:655
  111.8 1.7 %copy.22 = bf16[1,128,1024]{2,1,0:T(8,128)(2,1)} copy(bf16[1,128,1024]{2,1,0:T(8,128)(2,1)} %get-tuple-element.6) | data formatting | bytes 524288
  113.4 1.7 %copy.23 = bf16[1,128,1024]{2,1,0:T(8,128)(2,1)} copy(bf16[1,128,1024]{2,1,0:T(8,128)(2,1)} %get-tuple-element.7) | data formatting | bytes 524288
  115.1 1.7 %copy.24 = bf16[1,128,1024]{2,1,0:T(8,128)(2,1)} copy(bf16[1,128,1024]{2,1,0:T(8,128)(2,1)} %get-tuple-element.8) | data formatting | bytes 524288

commit v2 on v1

--- a/solution.py
+++ b/solution.py
@@ -16,8 +16,7 @@
 VOCAB = 1024
 TP = DT // 128
 SP = DS // 128
-CW = 256
-PPC = CW // 128
+CW = 128
 TCH = DT // CW
 SCH = DS // CW
 NCH = TCH + SCH
@@ -114,9 +113,8 @@
     shb,
     lens,
     align,
-    gq,
-    gk,
-    gv,
+    out,
+    grads,
     kv,
     qt,
     rt,
@@ -133,6 +131,7 @@
     post,
     ext,
     tail,
+    tail_in,
     lgrad,
     bias_t,
     bias_s,
@@ -140,6 +139,7 @@
     stat_c,
     stat,
     lsem,
+    osem,
     kv_send,
     kv_recv,
     q_send,
@@ -172,6 +172,11 @@
     yprev = lax.rem(s + ns - ystep, ns)
     s_next = lax.rem(s + 1, ns)
     s_prev = lax.rem(s + ns - 1, ns)
+    inside = s - y * ystep
+    znext = y * ystep + lax.rem(inside + 4, ystep)
+    zprev = y * ystep + lax.rem(inside + ystep - 4, ystep)
+    yp = lax.rem(y, 2)
+    zp = lax.rem(inside // 4, 2)
 
     own = [
         (tk.at[0], kv.at[0, pl.ds(CTX, R), pl.ds(0, DT)]),
@@ -200,135 +205,15 @@
         (g, behind),
         (g, ynext),
         (g, yprev),
+        (g, znext),
+        (g, zprev),
         (og, xdev),
         (og, s),
-        (og, s_next),
-        (og, s_prev),
+        (g, s_next),
+        (g, s_prev),
     ]
     for peer in peers:
         pl.semaphore_signal(barrier, inc=1, device_id=peer, device_id_type=MESH)
-    pl.semaphore_wait(barrier, len(peers))
-
-    def kv_place(dist, chunk):
-        return kv.at[:, cols(4 - dist, R), cols(chunk, CW)]
-
-    def q_place(dist, chunk):
-        return qm.at[0, cols(dist, R), :]
-
-    def m_place(dist, chunk):
-        return qm.at[1, cols(dist, R), cols(chunk, CW)]
-
-    def s_place(dist, chunk):
-        return stat.at[:, cols(dist, R)]
-
-    kvc = Cast(kv_place, kv_send, kv_recv, g, s, ahead, xdev, cdev, xl, core)
-    back = (g, s, behind, xdev, cdev, 1 - xl, 1 - core)
-    qc = Cast(q_place, q_send, q_recv, *back)
-    mc = Cast(m_place, m_send, m_recv, *back)
-    sc = Cast(s_place, s_send, s_recv, *back)
-
-    def piece(group, owner_y, of, lo=0, n=None):
-        depth = (DT if of < 2 else DS) // 16
-        half = (DT if of < 2 else DS) // 2
-        n = depth if n is None else n
-        first = group * half + (owner_y * 2 + core) * depth + lo
-        rows = pl.ds(pl.multiple_of(first, 16), n)
-        if of == 0:
-            return wt.at[rows, pl.ds(0, DT)]
-        if of == 1:
-            return wt.at[rows, pl.ds(DT, VOCAB)]
-        return ws.at[rows, :]
-
-    def across(i):
-        source = (tow, thw, sow, shw)[i]
-        depth = (DT if i < 2 else DS) // 16
-        half = (DT if i < 2 else DS) // 2
-        rows = pl.ds(pl.multiple_of((y * 2 + core) * depth, 16), depth)
-        there = pl.ds(pl.multiple_of(g * half + (y * 2 + core) * depth, 16), depth)
-        dest = (
-            wt.at[there, pl.ds(0, DT)],
-            wt.at[there, pl.ds(DT, VOCAB)],
-            ws.at[there, pl.ds(0, DS)],
-            ws.at[there, pl.ds(DS, VOCAB)],
-        )[i]
-        return pltpu.make_async_remote_copy(
-            src_ref=source.at[rows, :],
-            dst_ref=dest,
-            send_sem=wx_send.at[i],
-            recv_sem=wx_recv.at[i],
-            device_id=(og, xdev),
-            device_id_type=MESH,
-        )
-
-    def along(kind, of):
-        depth = (DT if of < 2 else DS) // 16
-        if kind < 2:
-            ref = piece(og, y, of)
-        elif kind == 2:
-            ref = piece(og, lax.rem(y + NY - 1, NY), of, 0, depth // 2)
-        else:
-            ref = piece(og, lax.rem(y + 1, NY), of, depth // 2, depth // 2)
-        return pltpu.make_async_remote_copy(
-            src_ref=ref,
-            dst_ref=ref,
-            send_sem=wy_send.at[kind, of],
-            recv_sem=wy_recv.at[kind, of],
-            device_id=(g, (ynext, yprev)[kind % 2]),
-            device_id_type=MESH,
-        )
-
-    def other_core(step, of):
-        ref = piece(og, lax.rem(y + step, NY), of)
-        return pltpu.make_async_remote_copy(
-            src_ref=ref,
-            dst_ref=ref,
-            send_sem=wc_send.at[step, of],
-            recv_sem=wc_recv.at[step, of],
-            device_id=(g, cdev),
-            device_id_type=MESH,
-        )
-
-    def w_first(of):
-        if of < 2:
-            across(of).wait_recv()
-        else:
-            across(2).wait_recv()
-            across(3).wait_recv()
-        along(0, of).start()
-        along(1, of).start()
-        other_core(0, of).start()
-
-    def w_second(of):
-        along(0, of).wait_recv()
-        along(1, of).wait_recv()
-        along(2, of).start()
-        along(3, of).start()
-        other_core(1, of).start()
-        other_core(3, of).start()
-
-    def w_third(of):
-        along(2, of).wait_recv()
-        along(3, of).wait_recv()
-        other_core(2, of).start()
-
-    def w_ready(of):
-        for step in range(NY):
-            other_core(step, of).wait_recv()
-
-    for i in range(4):
-        across(i).start()
-    local[0].wait()
-    local[1].wait()
-    for c in range(TCH):
-        kvc.start(c)
-    local[2].wait()
-    local[3].wait()
-    for c in range(TCH, NCH):
-        kvc.start(c)
-    local[4].wait()
-    qc.start(0)
-    for item in local[5:]:
-        item.wait()
 
     row = lax.broadcasted_iota(jnp.int32, (R, WIN), 0)
     col = lax.broadcasted_iota(jnp.int32, (R, WIN), 1)
@@ -343,6 +228,123 @@
     bias_k[...] = jnp.where(band & (first + col < ns * R) & (first + row < s_len), 0.0, FILL)
     stat_c[...] = jnp.zeros_like(stat_c)
 
+    pl.semaphore_wait(barrier, len(peers))
+
+    def kv_place(dist, chunk):
+        return kv.at[:, cols(4 - dist, R), cols(chunk, CW)]
+
+    def q_place(dist, chunk):
+        return qm.at[0, cols(dist, R), :]
+
+    def m_place(dist, chunk):
+        return qm.at[1, cols(dist, R), cols(chunk, CW)]
+
+    def s_place(dist, chunk):
+        return stat.at[:, cols(dist, R)]
+
+    kvc = Cast(kv_place, kv_send, kv_recv, g, s, ahead, xdev, cdev, xl, core)
+    back = (g, s, behind, xdev, cdev, 1 - xl, 1 - core)
+    qc = Cast(q_place, q_send, q_recv, *back)
+    mc = Cast(m_place, m_send, m_recv, *back)
+    sc = Cast(s_place, s_send, s_recv, *back)
+
+    def piece_rows(k, ypar, zpar):
+        if k < 4:
+            n = DT // 32
+            return (((ypar * 2 + zpar) * 2 + core) * 2 + k % 2) * n, n
+        n = DS // 8
+        return ((ypar, zpar)[k - 4] * 2 + core) * n, n
+
+    def piece(group, k, ypar, zpar):
+        first, n = piece_rows(k, ypar, zpar)
+        half = DT // 2 if k < 4 else DS // 2
+        rows = pl.ds(pl.multiple_of(group * half + first, 16), n)
+        if k < 4:
+            return wt.at[rows, (pl.ds(0, DT), pl.ds(DT, VOCAB))[k // 2]]
+        return ws.at[rows, (pl.ds(0, DS), pl.ds(DS, VOCAB))[k - 4]]
+
+    def across(k):
+        first, n = piece_rows(k, yp, zp)
+        source = (tow, tow, thw, thw, sow, shw)[k]
+        return pltpu.make_async_remote_copy(
+            src_ref=source.at[pl.ds(pl.multiple_of(first, 16), n), :],
+            dst_ref=piece(g, k, yp, zp),
+            send_sem=wx_send.at[k],
+            recv_sem=wx_recv.at[k],
+            device_id=(og, xdev),
+            device_id_type=MESH,
+        )
+
+    def along(k, kind):
+        if kind < 2:
+            ref, dev = piece(og, k, yp, zp), (yprev, zprev)[kind]
+        elif k % 2 == 0:
+            ref, dev = piece(og, k, yp, 1 - zp), yprev
+        else:
+            ref, dev = piece(og, k, 1 - yp, zp), zprev
+        return pltpu.make_async_remote_copy(
+            src_ref=ref,
+            dst_ref=ref,
+            send_sem=wy_send.at[kind, k],
+            recv_sem=wy_recv.at[kind, k],
+            device_id=(g, dev),
+            device_id_type=MESH,
+        )
+
+    def kinds(k):
+        return (0, 1) if k < 4 else (k - 4,)
+
+    def other_core(k, which):
+        ypar = 1 - yp if which in (1, 3) else yp
+        zpar = 1 - zp if which in (2, 3) else zp
+        ref = piece(og, k, ypar, zpar)
+        return pltpu.make_async_remote_copy(
+            src_ref=ref,
+            dst_ref=ref,
+            send_sem=wc_send.at[which, k],
+            recv_sem=wc_recv.at[which, k],
+            device_id=(g, cdev),
+            device_id_type=MESH,
+        )
+
+    def pieces(k):
+        return (0, 1, 2, 3) if k < 4 else (0, k - 3)
+
+    def w_first(k):
+        across(k).wait_recv()
+        for kind in kinds(k):
+            along(k, kind).start()
+        other_core(k, 0).start()
+
+    def w_second(k):
+        for kind in kinds(k):
+            along(k, kind).wait_recv()
+        if k < 4:
+            along(k, 2).start()
+        for kind in kinds(k):
+            other_core(k, 1 + kind).start()
+
+    def w_third(k):
+        along(k, 2).wait_recv()
+        other_core(k, 3).start()
+
+    def w_ready(k):
+        for which in pieces(k):
+            other_core(k, which).wait_recv()
+
+    for k in range(6):
+        across(k).start()
+    local[0].wait()
+    local[1].wait()
+    for c in range(TCH):
+        kvc.start(c)
+    local[2].wait()
+    local[3].wait()
+    for c in range(TCH, NCH):
+        kvc.start(c)
+    for item in local[4:]:
+        item.wait()
+
     lane = lax.broadcasted_iota(jnp.int32, (R, 128), 1)
     low = lane < 64
 
@@ -367,85 +369,68 @@
         o = o * inv.reshape(2 * R, 1)
         ctx_t[:, at] = merged(o).astype(BF16)
 
-    kvc.a(0)
-
-    def teacher_chunk(c, carry):
-        kvc.a(c + 1)
-        kvc.b(c)
-
-        @pl.when(c == 1)
-        def _():
-            w_first(0)
-
-        @pl.when(c == 2)
-        def _():
-            w_first(1)
-
-        @pl.when(c == 3)
-        def _():
-            w_second(0)
-
-        @pl.when(c == 4)
-        def _():
-            w_first(2)
-            w_third(0)
-
-        @pl.when(c == 5)
-        def _():
-            w_second(1)
-
-        kvc.c(c)
-        for i in range(PPC):
-            teacher_pair(c * PPC + i)
-        return carry
-
-    lax.fori_loop(0, TCH, teacher_chunk, 0)
-
-    def project(n, tiles, fn):
+    def project(lo, hi, fn):
         def body(i, carry):
             fn(i)
             return carry
 
-        lax.fori_loop(0, tiles, body, 0)
-
-    w_ready(0)
+        lax.fori_loop(lo, hi, body, 0)
+
+    kvc.a(0)
+
+    def at_step(i, steps):
+        for step, calls in steps.items():
+
+            @pl.when(i == step)
+            def _():
+                for call, k in calls:
+                    call(k)
+
+    def teacher_chunk(i, carry):
+        at_step(
+            i,
+            {
+                1: [(w_first, 0)],
+                3: [(w_first, 1), (w_second, 0)],
+                4: [(w_first, 2)],
+                6: [(w_first, 3), (w_second, 1)],
+                8: [(w_third, 0)],
+                10: [(w_second, 2), (w_third, 1), (w_first, 4)],
+                11: [(w_second, 3)],
+            },
+        )
+        kvc.a(i + 1)
+
+        @pl.when(i >= 1)
+        def _():
+            kvc.b(i - 1)
+
+        @pl.when(i >= 2)
+        def _():
+            kvc.c(i - 2)
+            teacher_pair(i - 2)
+
+        return carry
+
+    lax.fori_loop(0, TCH, teacher_chunk, 0)
+
+    def teacher_last(i, carry):
+        at_step(i, {TCH + 1: [(w_third, 2), (w_third, 3)]})
+        kvc.a(i + 1)
+        kvc.b(i - 1)
+        kvc.c(i - 2)
+        teacher_pair(i - 2)
+        return carry
+
+    lax.fori_loop(TCH, TCH + 2, teacher_last, 0)
 
     def t_hidden(i):
         at = cols(i, 256)
         hid[:, at] = (rt[:, at].astype(F32) + mm(ctx_t[...], wt[:, at])).astype(BF16)
 
-    project(0, DT // 256, t_hidden)
-    kvc.a(TCH + 1)
-    kvc.b(TCH)
-    w_third(1)
-    w_ready(1)
-
     def t_logits(i):
         at = cols(i, 256)
         logits[:, at] = mm(hid[...], wt[:, pl.ds(pl.multiple_of(DT + i * 256, 256), 256)]) + thb[:, at]
-
-    project(0, VOCAB // 256, t_logits)
-    x = logits[...]
-    e = jnp.exp(x - jnp.max(x, axis=-1, keepdims=True))
-    post[...] = (e * (1.0 / jnp.sum(e, axis=-1, keepdims=True))).astype(BF16)
-    to_body = pltpu.make_async_remote_copy(
-        src_ref=post,
-        dst_ref=ext,
-        send_sem=p_send.at[0],
-        recv_sem=p_recv.at[0],
-        device_id=(og, s),
-        device_id_type=MESH,
-    )
-    to_tail = pltpu.make_async_remote_copy(
-        src_ref=post.at[pl.ds(R - MAXD, MAXD), :],
-        dst_ref=tail.at[pl.ds(0, MAXD), :],
-        send_sem=p_send.at[1],
-        recv_sem=p_recv.at[1],
-        device_id=(og, s_next),
-        device_id_type=MESH,
-    )
-    to_body.start()
-    to_tail.start()
 
     def student_pair(j):
         at = cols(TP + j, 128)
@@ -464,43 +449,84 @@
         st = jnp.where(lane == 2 * j, lse[0], st)
         stat_c[...] = jnp.where(lane == 2 * j + 1, lse[1], st)
 
-    def student_chunk(c, carry):
-        @pl.when(c < NCH - 1)
-        def _():
-            kvc.a(c + 1)
-
-        kvc.b(c)
-
-        @pl.when(c == TCH + 1)
-        def _():
-            w_second(2)
-            qc.a(0)
-
-        @pl.when(c == TCH + 2)
-        def _():
-            qc.b(0)
-
-        @pl.when(c == TCH + 3)
-        def _():
-            w_third(2)
-
-        kvc.c(c)
-        for i in range(PPC):
-            student_pair((c - TCH) * PPC + i)
-        return carry
-
-    kvc.c(TCH)
-    for i in range(PPC):
-        student_pair(i)
-    lax.fori_loop(TCH + 1, NCH, student_chunk, 0)
-
+    def student_pairs(lo, hi):
+        def body(j, carry):
+            kvc.c(TCH + j)
+            student_pair(j)
+            return carry
+
+        lax.fori_loop(lo, hi, body, 0)
+
+    w_first(5)
+    kvc.a(TCH + 3)
+    kvc.b(TCH + 1)
+    w_ready(0)
+    w_ready(1)
+    project(0, 4, t_hidden)
+    kvc.a(TCH + 4)
+    kvc.b(TCH + 2)
+    project(4, DT // 256, t_hidden)
     w_ready(2)
+    w_ready(3)
+    project(0, 2, t_logits)
+    kvc.a(TCH + 5)
+    kvc.b(TCH + 3)
+    project(2, VOCAB // 256, t_logits)
+    x = logits[...]
+    e = jnp.exp(x - jnp.max(x, axis=-1, keepdims=True))
+    post[...] = (e * (1.0 / jnp.sum(e, axis=-1, keepdims=True))).astype(BF16)
+    to_body = pltpu.make_async_remote_copy(
+        src_ref=post,
+        dst_ref=ext,
+        send_sem=p_send.at[0],
+        recv_sem=p_recv.at[0],
+        device_id=(og, s),
+        device_id_type=MESH,
+    )
+    to_next = pltpu.make_async_remote_copy(
+        src_ref=post.at[pl.ds(R - MAXD, MAXD), :],
+        dst_ref=tail_in,
+        send_sem=p_send.at[1],
+        recv_sem=p_recv.at[1],
+        device_id=(g, s_next),
+        device_id_type=MESH,
+    )
+    to_tail = pltpu.make_async_remote_copy(
+        src_ref=tail_in,
+        dst_ref=tail.at[pl.ds(0, MAXD), :],
+        send_sem=p_send.at[2],
+        recv_sem=p_recv.at[2],
+        device_id=(og, s),
+        device_id_type=MESH,
+    )
+    to_next.start()
+    to_body.start()
+
+    qc.start(0)
+    kvc.a(TCH + 6)
+    kvc.b(TCH + 4)
+    student_pairs(0, 2)
+    to_next.wait_recv()
+    to_tail.start()
+    w_second(4)
+    kvc.a(TCH + 7)
+    kvc.b(TCH + 5)
+    student_pairs(2, 4)
+    kvc.b(TCH + 6)
+    student_pairs(4, 5)
+    w_second(5)
+    kvc.b(TCH + 7)
+    student_pairs(5, 6)
+    qc.a(0)
+    student_pairs(6, 8)
+    w_ready(4)
 
     def s_hidden(i):
         at = cols(i, 256)
         hid[:, at] = (rs[:, at].astype(F32) + mm(ctx_s[...], ws[:, at])).astype(BF16)
 
     project(0, DS // 256, s_hidden)
+    w_ready(5)
 
     def s_logits(i):
         at = cols(i, 256)
@@ -531,11 +557,12 @@
     project(0, DS // 256, s_hidden_grad)
 
     def s_mix_grad(i):
-        at = cols(i, CW)
+        at = cols(i, 256)
         qm[1, pl.ds(0, R), at] = mm(hid[:, pl.ds(0, DS)], ws[at, pl.ds(0, DS)], NT).astype(BF16)
-        mc.start(i)
-
-    project(0, DS // CW, s_mix_grad)
+        mc.start(2 * i)
+        mc.start(2 * i + 1)
+
+    project(0, DS // 256, s_mix_grad)
 
     def inner_pair(j, carry):
         at = cols(j, 128)
@@ -548,6 +575,7 @@
         stat_c[...] = jnp.where(lane == 17 + 2 * j, in1, st)
         return carry
 
+    qc.b(0)
     lax.fori_loop(0, SP, inner_pair, 0)
     stat[:, pl.ds(0, R)] = stat_c[...].T[:32]
     sc.start(0)
@@ -563,31 +591,7 @@
         in1 = jnp.sum(jnp.where(lane == 17 + 2 * j, st, zero), axis=-1, keepdims=True)
         inner = jnp.concatenate([in0[None], in1[None]], axis=0)
         ds = (probs[j] * (dp - inner)).astype(BF16).reshape(2 * R, WIN)
-        gq[0, :, at] = (merged(mm(ds, kv[0, :, kat])) * 0.125).astype(BF16)
-
-    def query_chunk(c, carry):
-        for i in range(PPC):
-            query_pair(c * PPC + i)
-        mc.a(c)
-
-        @pl.when(c == 0)
-        def _():
-            sc.a(0)
-
-        @pl.when(c == 1)
-        def _():
-            sc.b(0)
-
-        @pl.when(c > 0)
-        def _():
-            mc.b(c - 1)
-
-        return carry
-
-    lax.fori_loop(0, SCH, query_chunk, 0)
-    mc.b(SCH - 1)
-    qc.c(0)
-    sc.c(0)
+        grads[0, :, at] = (merged(mm(ds, kv[0, :, kat])) * 0.125).astype(BF16)
 
     def key_pair(j):
         at = cols(j, 128)
@@ -600,18 +604,60 @@
             [stat[pl.ds(16 + 2 * j, 1), :][None], stat[pl.ds(17 + 2 * j, 1), :][None]], 0
         )
         pr = jnp.exp(x - lse)
-        gv[0, :, at] = merged(mm(pr.astype(BF16).reshape(2 * R, WIN), m)).astype(BF16)
+        grads[2, :, at] = merged(mm(pr.astype(BF16).reshape(2 * R, WIN), m)).astype(BF16)
         dp = mm(stacked(kv[1, pl.ds(CTX, R), kat]), m, NT).reshape(2, R, WIN)
         ds = (pr * (dp - inner)).astype(BF16).reshape(2 * R, WIN)
-        gk[0, :, at] = (merged(mm(ds, q)) * 0.125).astype(BF16)
-
-    def key_chunk(c, carry):
-        mc.c(c)
-        for i in range(PPC):
-            key_pair(c * PPC + i)
+        grads[1, :, at] = (merged(mm(ds, q)) * 0.125).astype(BF16)
+
+    def result(i, j):
+        at = cols(j, 128)
+        return pltpu.make_async_copy(grads.at[i, :, at], out.at[i, :, at], osem.at[i, j])
+
+    def key_step(j):
+        mc.c(j)
+        key_pair(j)
+        result(1, j).start()
+        result(2, j).start()
+
+    def last_chunk(i, carry):
+        query_pair(i)
+        result(0, i).start()
+        mc.a(i)
+
+        @pl.when(i == 1)
+        def _():
+            sc.a(0)
+
+        @pl.when(i >= 3)
+        def _():
+            mc.b(i - 3)
+
+        @pl.when(i == 4)
+        def _():
+            sc.b(0)
+            qc.c(0)
+
+        @pl.when(i == 5)
+        def _():
+            sc.c(0)
+
+        @pl.when(i >= 5)
+        def _():
+            key_step(i - 5)
+
         return carry
 
-    lax.fori_loop(0, SCH, key_chunk, 0)
+    lax.fori_loop(0, SP, last_chunk, 0)
+
+    def rest(i, carry):
+        @pl.when(i < 6)
+        def _():
+            mc.b(i + 2)
+
+        key_step(i)
+        return carry
+
+    lax.fori_loop(3, SP, rest, 0)
 
     def kv_sent(c, carry):
         kvc.sent(c)
@@ -624,17 +670,23 @@
         return carry
 
     lax.fori_loop(0, SCH, m_sent, 0)
+    def results(j, carry):
+        for i in range(3):
+            result(i, j).wait()
+        return carry
+
+    lax.fori_loop(0, SP, results, 0)
     qc.sent(0)
     sc.sent(0)
     to_body.wait_send()
+    to_next.wait_send()
     to_tail.wait_send()
-    for i in range(4):
-        across(i).wait_send()
-    for of in range(3):
-        for kind in range(4):
-            along(kind, of).wait_send()
-        for step in range(NY):
-            other_core(step, of).wait_send()
+    for k in range(6):
+        across(k).wait_send()
+        for kind in (0, 1, 2) if k < 4 else kinds(k):
+            along(k, kind).wait_send()
+        for which in pieces(k):
+            other_core(k, which).wait_send()
 
 
 def on_device(*args):
@@ -650,14 +702,15 @@
     in_specs[13] = vmem
     in_specs[14] = smem
     in_specs[15] = vmem
-    out = jax.ShapeDtypeStruct((1, R, DS), BF16)
+    out = jax.ShapeDtypeStruct((3, R, DS), BF16)
     dma = pltpu.SemaphoreType.DMA
-    return pl.pallas_call(
+    grads = pl.pallas_call(
         functools.partial(kernel, ns),
-        out_shape=(out, out, out),
+        out_shape=out,
         in_specs=in_specs,
-        out_specs=(vmem, vmem, vmem),
+        out_specs=hbm,
         scratch_shapes=[
+            pltpu.VMEM((3, R, DS), BF16),
             pltpu.VMEM((2, WIN, DT + DS), BF16),
             pltpu.VMEM((R, DT), BF16),
             pltpu.VMEM((R, DT), BF16),
@@ -674,6 +727,7 @@
             pltpu.VMEM((R, VOCAB), BF16),
             pltpu.VMEM((R, VOCAB), BF16),
             pltpu.VMEM((R, VOCAB), BF16),
+            pltpu.VMEM((MAXD, VOCAB), BF16),
             pltpu.VMEM((R, VOCAB), BF16),
             pltpu.VMEM((R, WIN), F32),
             pltpu.VMEM((R, WIN), F32),
@@ -681,6 +735,7 @@
             pltpu.VMEM((R, 128), F32),
             pltpu.VMEM((32, WIN), F32),
             dma((12,)),
+            dma((3, SP)),
             dma((4, NCH)),
             dma((4, NCH)),
             dma((4, 1)),
@@ -689,19 +744,20 @@
             dma((4, SCH)),
             dma((4, 1)),
             dma((4, 1)),
-            dma((4,)),
-            dma((4,)),
-            dma((4, 3)),
-            dma((4, 3)),
-            dma((4, 3)),
-            dma((4, 3)),
-            dma((2,)),
-            dma((2,)),
+            dma((6,)),
+            dma((6,)),
+            dma((3, 6)),
+            dma((3, 6)),
+            dma((4, 6)),
+            dma((4, 6)),
+            dma((3,)),
+            dma((3,)),
         ],
         compiler_params=pltpu.CompilerParams(
             collective_id=0, has_side_effects=True, vmem_limit_bytes=56 * 1024 * 1024
         ),
     )(*args)
+    return grads[0:1], grads[1:2], grads[2:3]
 
 
 def solution(mesh):

time: 117 us -> 83.9 us (0.72)
  Pallas kernels: 111 us -> 81.1 us
  local copies, waits for them, and re-layouts: 5.01 us -> 2 us
    pallas_call x1, Pallas kernels: 111 us -> 81.1 us  [on_device(): pl.pallas_call(functools.partial(kernel, ns), out_shape=out, in_specs=in_...]
    unnamed x3 -> x0, local copies, waits for them, and re-layouts: 5.01 us -> none
    slice x0 -> x1, local copies, waits for them, and re-layouts: none -> 2 us  [on_device(): return (grads[0:1], grads[1:2], grads[2:3])]
where the time goes in v2:
time: 83.9 us; the launch traced here: 83.8 us
  Pallas kernels  81.1 us (97%)
  local copies, waits for them, and re-layouts  2 us (2%)
    pallas_call x1, Pallas kernels, on_device(): pl.pallas_call(functools.partial(kernel, ns), out_shape=out, in_specs=in_...  81.1 us
    slice x1, local copies, waits for them, and re-layouts, on_device(): return (grads[0:1], grads[1:2], grads[2:3])  2 us

profile of v2, /device:TPU:1, one launch (start us, length us, event | category | flops | bytes accessed | tf_op | source)
XLA Modules:
  0.0 83.8 jit_solution(17677141167766879282)
XLA Ops:
  0.6 81.1 %shard_map.175 = bf16[3,128,1024]{2,1,0:T(8,128)(2,1)} custom-call(bf16[1,128,1536]{2,1,0:T(8,128)(2,1)} %tq.1, bf16[1,128,1536]{2,1,0:T(8,128)(2,1)} %tk.1, bf16[1,128,1536]{2,1,0:T(8,128)(2,1)} %tv.1, bf16[1,128,1536]{2,1,0:T(8,128)(2,1)} %tr.1, bf16[768,1536]{1,0:T(8,128)(2,1)} %tow.1, bf16[768,1024]{1,0:T(8,128)(2,1)} %thw.1, f32[1,1024]{1,0:T(1,128)} %bitcast.2, ...), custom_call_target="tpu_custom_call" | custom-call | tf_op jit(solution)/shard_map/pallas_call | solution.py:707
  81.8 2.0 %fusion = (bf16[1,128,1024]{2,1,0:T(8,128)(2,1)}, bf16[1,128,1024]{2,1,0:T(8,128)(2,1)}, bf16[1,128,1024]{2,1,0:T(8,128)(2,1)}) fusion(bf16[3,128,1024]{2,1,0:T(8,128)(2,1)} %shard_map.175), kind=kLoop, calls=%fused_computation | loop fusion | bytes 1572864 | tf_op jit(solution)/shard_map/slice | solution.py:760

commit v3 on v2

--- a/solution.py
+++ b/solution.py
@@ -130,7 +130,6 @@
     logits,
     post,
     ext,
-    tail,
     tail_in,
     lgrad,
     bias_t,
@@ -195,7 +194,7 @@
     local = [pltpu.make_async_copy(a, b, lsem.at[i]) for i, (a, b) in enumerate(own)]
     for item in local:
         item.start()
-    tail[pl.ds(MAXD, R - MAXD), :] = jnp.zeros((R - MAXD, VOCAB), BF16)
+    ext[pl.ds(R + MAXD, R - MAXD), :] = jnp.zeros((R - MAXD, VOCAB), BF16)
 
     barrier = pltpu.get_barrier_semaphore()
     peers = [
@@ -450,12 +449,10 @@
         stat_c[...] = jnp.where(lane == 2 * j + 1, lse[1], st)
 
     def student_pairs(lo, hi):
-        def body(j, carry):
+        for j in range(lo, hi):
             kvc.c(TCH + j)
+        for j in range(lo, hi):
             student_pair(j)
-            return carry
-
-        lax.fori_loop(lo, hi, body, 0)
 
     w_first(5)
     kvc.a(TCH + 3)
@@ -477,7 +474,7 @@
     post[...] = (e * (1.0 / jnp.sum(e, axis=-1, keepdims=True))).astype(BF16)
     to_body = pltpu.make_async_remote_copy(
         src_ref=post,
-        dst_ref=ext,
+        dst_ref=ext.at[pl.ds(0, R), :],
         send_sem=p_send.at[0],
         recv_sem=p_recv.at[0],
         device_id=(og, s),
@@ -493,14 +490,13 @@
     )
     to_tail = pltpu.make_async_remote_copy(
         src_ref=tail_in,
-        dst_ref=tail.at[pl.ds(0, MAXD), :],
+        dst_ref=ext.at[pl.ds(R, MAXD), :],
         send_sem=p_send.at[2],
         recv_sem=p_recv.at[2],
         device_id=(og, s),
         device_id_type=MESH,
     )
     to_next.start()
-    to_body.start()
 
     qc.start(0)
     kvc.a(TCH + 6)
@@ -510,14 +506,13 @@
     to_tail.start()
     w_second(4)
     kvc.a(TCH + 7)
+    to_body.start()
     kvc.b(TCH + 5)
     student_pairs(2, 4)
     kvc.b(TCH + 6)
-    student_pairs(4, 5)
+    student_pairs(4, 6)
     w_second(5)
     kvc.b(TCH + 7)
-    student_pairs(5, 6)
-    qc.a(0)
     student_pairs(6, 8)
     w_ready(4)
 
@@ -539,16 +534,19 @@
     pick_body = jnp.where(rows == lane, 1.0, 0.0).astype(BF16)
     pick_tail = jnp.where(rows + MAXD == lane, 1.0, 0.0)
     pick_tail = jnp.where(lane < MAXD, pick_tail, 0.0).astype(BF16)
-    to_body.wait_recv()
-    to_tail.wait_recv()
-    targets = mm(pick_body, ext[...]) + mm(pick_tail, tail[...])
+    pick = jnp.concatenate([pick_body, pick_tail], axis=1)
     x = logits[...]
     e = jnp.exp(x - jnp.max(x, axis=-1, keepdims=True))
     predicted = e * (1.0 / jnp.sum(e, axis=-1, keepdims=True))
     frame = first + lax.broadcasted_iota(jnp.int32, (R, 1), 0)
     valid = jnp.where(frame < s_len, 16.0, 0.0)
+    to_body.wait_recv()
+    to_tail.wait_recv()
+    targets = mm(pick, ext[...])
     total = jnp.sum(targets, axis=-1, keepdims=True)
     lgrad[...] = (valid * (total * predicted - targets)).astype(BF16)
+
+    qc.a(0)
 
     def s_hidden_grad(i):
         at = cols(i, 256)
@@ -558,27 +556,33 @@
 
     def s_mix_grad(i):
         at = cols(i, 256)
-        qm[1, pl.ds(0, R), at] = mm(hid[:, pl.ds(0, DS)], ws[at, pl.ds(0, DS)], NT).astype(BF16)
-        mc.start(2 * i)
-        mc.start(2 * i + 1)
+        m = mm(hid[:, pl.ds(0, DS)], ws[at, pl.ds(0, DS)], NT).astype(BF16)
+        qm[1, pl.ds(0, R), at] = m
+        prod = m.astype(F32) * mix_s[:, at]
+        st = stat_c[...]
+        for p in range(2):
+            part = prod[:, p * 128 : (p + 1) * 128]
+            zero = jnp.zeros_like(part)
+            in0 = jnp.sum(jnp.where(low, part, zero), axis=-1, keepdims=True)
+            in1 = jnp.sum(jnp.where(low, zero, part), axis=-1, keepdims=True)
+            st = jnp.where(lane == 16 + 4 * i + 2 * p, in0, st)
+            st = jnp.where(lane == 17 + 4 * i + 2 * p, in1, st)
+        stat_c[...] = st
+
+        @pl.when(i == 0)
+        def _():
+            mc.start(0)
+            mc.start(1)
+
+        @pl.when(i == 1)
+        def _():
+            mc.start(2)
 
     project(0, DS // 256, s_mix_grad)
-
-    def inner_pair(j, carry):
-        at = cols(j, 128)
-        prod = qm[1, pl.ds(0, R), at].astype(F32) * mix_s[:, at]
-        zero = jnp.zeros_like(prod)
-        in0 = jnp.sum(jnp.where(low, prod, zero), axis=-1, keepdims=True)
-        in1 = jnp.sum(jnp.where(low, zero, prod), axis=-1, keepdims=True)
-        st = stat_c[...]
-        st = jnp.where(lane == 16 + 2 * j, in0, st)
-        stat_c[...] = jnp.where(lane == 17 + 2 * j, in1, st)
-        return carry
-
-    qc.b(0)
-    lax.fori_loop(0, SP, inner_pair, 0)
     stat[:, pl.ds(0, R)] = stat_c[...].T[:32]
     sc.start(0)
+    for c in range(3, SCH):
+        mc.start(c)
 
     def query_pair(j):
         at = cols(j, 128)
@@ -613,18 +617,31 @@
         at = cols(j, 128)
         return pltpu.make_async_copy(grads.at[i, :, at], out.at[i, :, at], osem.at[i, j])
 
-    def key_step(j):
-        mc.c(j)
-        key_pair(j)
-        result(1, j).start()
-        result(2, j).start()
+    def query_step(first_pair, count):
+        for p in range(count):
+            query_pair(first_pair + p)
+        for p in range(count):
+            result(0, first_pair + p).start()
+
+    def key_step(first_pair, count):
+        for p in range(count):
+            mc.c(first_pair + p)
+        for p in range(count):
+            key_pair(first_pair + p)
+        for p in range(count):
+            result(1, first_pair + p).start()
+            result(2, first_pair + p).start()
 
     def last_chunk(i, carry):
-        query_pair(i)
-        result(0, i).start()
+        query_step(i * 2, 2)
+        for p in range(2):
+            relay_step(i * 2 + p)
+        return carry
+
+    def relay_step(i):
         mc.a(i)
 
-        @pl.when(i == 1)
+        @pl.when(i == 2)
         def _():
             sc.a(0)
 
@@ -632,32 +649,26 @@
         def _():
             mc.b(i - 3)
 
-        @pl.when(i == 4)
+        @pl.when(i == 5)
         def _():
             sc.b(0)
-            qc.c(0)
-
-        @pl.when(i == 5)
+
+    lax.fori_loop(0, SP // 2, last_chunk, 0)
+    mc.b(5)
+    qc.b(0)
+    sc.c(0)
+    qc.c(0)
+
+    def rest(i, carry):
+        key_step(i * 2, 2)
+
+        @pl.when(i < 2)
         def _():
-            sc.c(0)
-
-        @pl.when(i >= 5)
-        def _():
-            key_step(i - 5)
+            mc.b(i + 6)
 
         return carry
 
-    lax.fori_loop(0, SP, last_chunk, 0)
-
-    def rest(i, carry):
-        @pl.when(i < 6)
-        def _():
-            mc.b(i + 2)
-
-        key_step(i)
-        return carry
-
-    lax.fori_loop(3, SP, rest, 0)
+    lax.fori_loop(0, SP // 2, rest, 0)
 
     def kv_sent(c, carry):
         kvc.sent(c)
@@ -725,8 +736,7 @@
             pltpu.VMEM((R, DT), BF16),
             pltpu.VMEM((R, VOCAB), F32),
             pltpu.VMEM((R, VOCAB), BF16),
-            pltpu.VMEM((R, VOCAB), BF16),
-            pltpu.VMEM((R, VOCAB), BF16),
+            pltpu.VMEM((2 * R, VOCAB), BF16),
             pltpu.VMEM((MAXD, VOCAB), BF16),
             pltpu.VMEM((R, VOCAB), BF16),
             pltpu.VMEM((R, WIN), F32),

time: 83.9 us -> 82.3 us (0.981)
  Pallas kernels: 81.1 us -> 79.5 us
    pallas_call x1, Pallas kernels: 81.1 us -> 79.5 us  [on_device(): pl.pallas_call(functools.partial(kernel, ns), out_shape=out, in_specs=in_...]
where the time goes in v3:
time: 82.3 us; the launch traced here: 82.2 us
  Pallas kernels  79.5 us (97%)
  local copies, waits for them, and re-layouts  2 us (2%)
    pallas_call x1, Pallas kernels, on_device(): pl.pallas_call(functools.partial(kernel, ns), out_shape=out, in_specs=in_...  79.5 us
    slice x1, local copies, waits for them, and re-layouts, on_device(): return (grads[0:1], grads[1:2], grads[2:3])  2 us

profile of v3, /device:TPU:1, one launch (start us, length us, event | category | flops | bytes accessed | tf_op | source)
XLA Modules:
  0.0 82.2 jit_solution(1304615863652085085)
XLA Ops:
  0.6 79.5 %shard_map.175 = bf16[3,128,1024]{2,1,0:T(8,128)(2,1)} custom-call(bf16[1,128,1536]{2,1,0:T(8,128)(2,1)} %tq.1, bf16[1,128,1536]{2,1,0:T(8,128)(2,1)} %tk.1, bf16[1,128,1536]{2,1,0:T(8,128)(2,1)} %tv.1, bf16[1,128,1536]{2,1,0:T(8,128)(2,1)} %tr.1, bf16[768,1536]{1,0:T(8,128)(2,1)} %tow.1, bf16[768,1024]{1,0:T(8,128)(2,1)} %thw.1, f32[1,1024]{1,0:T(1,128)} %bitcast.2, ...), custom_call_target="tpu_custom_call" | custom-call | tf_op jit(solution)/shard_map/pallas_call | solution.py:718
  80.2 2.0 %fusion = (bf16[1,128,1024]{2,1,0:T(8,128)(2,1)}, bf16[1,128,1024]{2,1,0:T(8,128)(2,1)}, bf16[1,128,1024]{2,1,0:T(8,128)(2,1)}) fusion(bf16[3,128,1024]{2,1,0:T(8,128)(2,1)} %shard_map.175), kind=kLoop, calls=%fused_computation | loop fusion | bytes 1572864 | tf_op jit(solution)/shard_map/slice | solution.py:770
